TPU v7x, 128 devices: a whole 4x4x4 slice. The times are simulated.
128 devices in a mesh: gx: 16 (over z, x), gy: 8 (over y, core).
Axes of the slice: x: 4, y: 4, z: 4, core: 2. Of those that a mesh axis runs over, the one named last changes fastest.
Arguments:
- potential_warmth: float32 [2304, 30, 3000], P(('gx', 'gy')), may hold values from -6 to 6
- saltiness_anomaly: float32 [2304, 30, 3000], P(('gx', 'gy')), may hold values from -6 to 6
- topmost_thermal_inflow: float32 [2304, 3000], P(('gx', 'gy')), may hold values from -8 to 8
- diffusivity_factor: float32 [29], replicated, may hold values from 0.05 to 5
- place_tile_number: int32 [2304], P(('gx', 'gy')), may hold values from -1 to 2303, as said below
- place_stack_strata: int32 [2304, 3000], P(('gx', 'gy')), may hold values from 0 to 30, as said below
- mesh_stack_strata: int32 [2400, 2880], P('gy', 'gx'), may hold values from 0 to 30, as said below
Outputs:
- temperature_new: float32 [2304, 30, 3000], P(('gx', 'gy'))
- salinity_new: float32 [2304, 30, 3000], P(('gx', 'gy'))
- surface_height: float32 [2400, 2880], P('gy', 'gx')
- misfit_vector: float32 [2400, 2880], P('gy', 'gx')
Inputs may be any that keep to these rules, and one draw needn't show every extreme that they name: `place_tile_number`: block (by, bx) has id by * 48 + bx. Every block holding an ocean column (mesh_stack_strata > 0) sits in exactly one slot, no block twice, and unlisted blocks are all land. The device at gx, gy holds only blocks with by // 6 = gy, and at most 2 blocks with the same bx // 3; some device holds exactly 2 such blocks. `place_stack_strata`: entry i * 60 + j of a slot equals mesh_stack_strata at row by * 50 + i, column bx * 60 + j of the slot's block; empty slots hold zeros. `mesh_stack_strata`: zero on land.
All inputs are finite; a program needn't handle non-finite values.
Results may differ from a plain program's by a relative error of at most 0.0003.
Values sent between devices are 32-bit elements; how exact they have to be, the bound alone decides.
A program may use at most 256 MiB of HBM per device.

v0:
```python
import jax
import jax.numpy as jnp
from jax import lax
from jax.sharding import PartitionSpec as P

TILE_SPAN_EASTWARD = 60
TILE_SPAN_NORTH = 50
KX = 3
KY = 6
SEA_DEPTH_STRATA = 30
ITERS = 3


HALINE_CONTRACT = 0.8
THERMAL_EXPANSE = 0.6
DAMPING = 0.05


def swapped(value, axis, bit):
    mask = 2**bit
    pairs = [(source, source ^ mask) for source in range(lax.axis_size(axis))]
    return lax.ppermute(value, axis, pairs)


def with_halo(cells, sides, width):
    for axis, dim in sides:
        count = lax.axis_size(axis)
        head = lax.slice_in_dim(cells, 0, width, axis=dim)
        tail = lax.slice_in_dim(cells, cells.shape[dim] - width, cells.shape[dim], axis=dim)
        cells = jnp.concatenate(
            [
                lax.ppermute(tail, axis, [(i, (i + 1) % count) for i in range(count)]),
                cells,
                lax.ppermute(head, axis, [((i + 1) % count, i) for i in range(count)]),
            ],
            axis=dim,
        )
    return cells


def thomas_vertical_inverse(
    potential_warmth,
    saltiness_anomaly,
    topmost_thermal_inflow,
    diffusivity_factor,
    marine_strata_number,
):
    wet_strata_number = potential_warmth.shape[1]
    coupling = [
        jnp.where(
            stratum_position + 1 < marine_strata_number, diffusivity_factor[stratum_position], 0.0
        )
        for stratum_position in range(wet_strata_number - 1)
    ]
    forced = jnp.where(marine_strata_number > 0, topmost_thermal_inflow, 0.0)
    gains = []
    heat_rows = []
    salt_rows = []
    for stratum_position in range(wet_strata_number):
        pivots = jnp.ones(topmost_thermal_inflow.shape, jnp.float32)
        thermal_forcing_part = potential_warmth[:, stratum_position, :]
        salt_term = saltiness_anomaly[:, stratum_position, :]
        if stratum_position == 0:
            thermal_forcing_part = thermal_forcing_part + forced
        if stratum_position + 1 < wet_strata_number:
            pivots = pivots + coupling[stratum_position]
        if stratum_position > 0:
            pivots = (
                pivots
                + coupling[stratum_position - 1]
                - coupling[stratum_position - 1] * gains[stratum_position - 1]
            )
            thermal_forcing_part = (
                thermal_forcing_part
                + coupling[stratum_position - 1] * heat_rows[stratum_position - 1]
            )
            salt_term = salt_term + coupling[stratum_position - 1] * salt_rows[stratum_position - 1]
        if stratum_position + 1 < wet_strata_number:
            gains.append(coupling[stratum_position] / pivots)
        else:
            gains.append(jnp.zeros_like(pivots))
        heat_rows.append(thermal_forcing_part / pivots)
        salt_rows.append(salt_term / pivots)
    heat_out = [heat_rows[wet_strata_number - 1]]
    salt_out = [salt_rows[wet_strata_number - 1]]
    for stratum_position in range(wet_strata_number - 2, -1, -1):
        heat_out.append(heat_rows[stratum_position] + gains[stratum_position] * heat_out[-1])
        salt_out.append(salt_rows[stratum_position] + gains[stratum_position] * salt_out[-1])
    return (jnp.stack(heat_out[::-1], axis=1), jnp.stack(salt_out[::-1], axis=1))


def weight_balanced(revised_warmth, revised_saltiness, marine_strata_number):
    running = jnp.zeros(marine_strata_number.shape, jnp.float32)
    layers_out = []
    for stratum_position in range(revised_warmth.shape[1]):
        mass_per_volume = jnp.where(
            stratum_position < marine_strata_number,
            HALINE_CONTRACT * revised_saltiness[:, stratum_position, :]
            - THERMAL_EXPANSE * revised_warmth[:, stratum_position, :],
            0.0,
        )
        running = running + mass_per_volume
        layers_out.append(running)
    return jnp.stack(layers_out, axis=1)


def locate(keys, wanted):
    matches = keys[None, :] == wanted[:, None]
    indices = jnp.arange(keys.shape[0], dtype=jnp.int32)
    return (jnp.sum(jnp.where(matches, indices[None, :], 0), axis=1), jnp.any(matches, axis=1))


def to_region(blocks):
    wet_strata_number = blocks.shape[1]
    shaped = blocks.reshape(
        KY, KX, wet_strata_number, TILE_SPAN_NORTH, TILE_SPAN_EASTWARD
    ).transpose(2, 0, 3, 1, 4)
    return shaped.reshape(wet_strata_number, KY * TILE_SPAN_NORTH, KX * TILE_SPAN_EASTWARD)


def fold_rows(rows):
    partner = rows
    for bit_index in range(lax.axis_size("gx").bit_length() - 1):
        partner = swapped(partner, "gx", bit_index)
    return partner[:, ::-1]


def sides(field, padded, folded, index_y, span_y):
    east_side = padded[:, 1:-1, 2:]
    west_side = padded[:, 1:-1, :-2]
    north_row = jnp.where(index_y == span_y - 1, folded, padded[:, -1, 1:-1])
    south_row = jnp.where(index_y == 0, 0.0, padded[:, 0, 1:-1])
    north_side = jnp.concatenate([field[:, 1:, :], north_row[:, None, :]], axis=1)
    south_side = jnp.concatenate([south_row[:, None, :], field[:, :-1, :]], axis=1)
    return (east_side, west_side, north_side, south_side)


def global_sum(values):
    return lax.psum(jnp.sum(values), ("gx", "gy"))


def on_device(
    potential_warmth,
    saltiness_anomaly,
    topmost_thermal_inflow,
    diffusivity_factor,
    place_tile_number,
    place_stack_strata,
    mesh_stack_strata,
):
    revised_warmth, revised_saltiness = thomas_vertical_inverse(
        potential_warmth,
        saltiness_anomaly,
        topmost_thermal_inflow,
        diffusivity_factor,
        place_stack_strata,
    )
    normal_stress = weight_balanced(revised_warmth, revised_saltiness, place_stack_strata)
    span_x = lax.axis_size("gx")
    span_y = lax.axis_size("gy")
    index_x = lax.axis_index("gx")
    index_y = lax.axis_index("gy")
    capacity = (KX * KY + span_x - 1) // span_x
    blocks_x = KX * span_x
    slot_count = place_tile_number.shape[0]
    rows_out = span_x * capacity
    valid = place_tile_number >= 0
    owner_x = jnp.where(valid, jnp.maximum(place_tile_number, 0) % blocks_x // KX, -1)
    slot_order = jnp.arange(slot_count)
    earlier = (owner_x[None, :] == owner_x[:, None]) & (slot_order[None, :] < slot_order[:, None])
    ranking = jnp.sum(earlier.astype(jnp.int32), axis=1)
    send_row = jnp.where(valid, owner_x * capacity + ranking, -1)
    source, filled = locate(send_row, jnp.arange(rows_out, dtype=jnp.int32))
    send_ids = jnp.where(filled, place_tile_number[source], -1)
    wanted = (index_y * KY + slot_order // KX) * blocks_x + index_x * KX + slot_order % KX
    region_rows = mesh_stack_strata.shape[0]
    region_cols = mesh_stack_strata.shape[1]
    send_cols = jnp.where(filled[:, None, None], jnp.take(normal_stress, source, axis=0), 0.0)
    got_cols, got_ids = (
        lax.all_to_all(send_cols, "gx", split_axis=0, concat_axis=0, tiled=True),
        lax.all_to_all(send_ids, "gx", split_axis=0, concat_axis=0, tiled=True),
    )
    spots, found = locate(got_ids, wanted)
    placed = jnp.where(found[:, None, None], jnp.take(got_cols, spots, axis=0), 0.0)
    region = to_region(placed)
    partial_value = jnp.zeros((region_rows, region_cols), jnp.float32)
    boundary = (1.0, 1.0, 1.0, 1.0)
    depth = mesh_stack_strata.astype(jnp.float32)
    stacked = jnp.concatenate([region, depth[None]], axis=0)
    folded_top = fold_rows(stacked[:, -1, :])
    padded = with_halo(stacked, (("gy", 1), ("gx", 2)), 1)
    beside_all = sides(stacked, padded, folded_top, index_y, span_y)
    layer_index = jnp.arange(SEA_DEPTH_STRATA, dtype=jnp.float32)[:, None, None]
    rhs = partial_value
    weights = []
    for neighbour, edge_mask in zip(beside_all, boundary):
        face_levels = jnp.minimum(depth, neighbour[-1])
        face_flux = jnp.sum(
            jnp.where(layer_index < face_levels, neighbour[:-1] - region, 0.0), axis=0
        )
        rhs = rhs + face_flux * edge_mask
        weights.append(face_levels / SEA_DEPTH_STRATA)
    rhs = rhs / SEA_DEPTH_STRATA
    damping = jnp.where(depth > 0, DAMPING, 1.0)
    diagonal = damping + weights[0] + weights[1] + weights[2] + weights[3]
    elevation = jnp.zeros((region_rows, region_cols), jnp.float32)
    misfit_vector = rhs
    precond = misfit_vector / diagonal
    direction = precond
    precond_dot = global_sum(misfit_vector * precond)
    for iteration in range(ITERS):
        field_pad = with_halo(direction[None], (("gy", 1), ("gx", 2)), 1)
        field_fold = fold_rows(direction[-1:, :])
        result = damping * direction
        for operate_neighbour, weight in zip(
            sides(direction[None], field_pad, field_fold, index_y, span_y), weights
        ):
            result = result + weight * (direction - operate_neighbour[0])
        step_size = precond_dot / lax.psum(jnp.sum(direction * result), ("gx", "gy"))
        elevation = elevation + step_size * direction
        misfit_vector = misfit_vector - step_size * result
        precond = misfit_vector / diagonal
        next_dot = global_sum(misfit_vector * precond)
        direction = precond + next_dot / precond_dot * direction
        precond_dot = next_dot
    return (revised_warmth, revised_saltiness, elevation, misfit_vector)


def solution(mesh):
    in_specs = (
        P(("gx", "gy"), None, None),
        P(("gx", "gy"), None, None),
        P(("gx", "gy"), None),
        P(),
        P(("gx", "gy")),
        P(("gx", "gy"), None),
        P("gy", "gx"),
    )
    out_specs = (
        P(("gx", "gy"), None, None),
        P(("gx", "gy"), None, None),
        P("gy", "gx"),
        P("gy", "gx"),
    )
    return jax.shard_map(
        on_device, mesh=mesh, in_specs=in_specs, out_specs=out_specs, check_vma=False
    )
```

profile of v0, /device:TPU:1, one launch (start us, length us, event | category | flops | bytes accessed | tf_op | source)
XLA Modules:
  0.0 985.9 jit_solution(9361579842542974251)
XLA Ops:
  5.0 8.4 all-to-all-start
  13.5 9.9 %fusion.305 = (f32[18,1,3000]{2,1,0:T(1,128)S(1)}, f32[18,1,3000]{2,1,0:T(1,128)S(1)}, f32[18,1,3000]{2,1,0:T(1,128)S(1)}, f32[18,1,3000]{2,1,0:T(1,128)S(1)}, f...) fusion(f32[18,30,3000]{2,1,0:T(8,128)} %param.8), kind=kLoop, calls=%fused_computation.766 | loop fusion | bytes 4752000 | tf_op jit(solution)/shard_map/slice | solution.py:62
  23.4 16.4 %fusion.304 = (f32[18,1,3000]{2,1,0:T(1,128)}, f32[18,1,3000]{2,1,0:T(1,128)S(1)}, f32[18,1,3000]{2,1,0:T(1,128)S(1)}, f32[18,1,3000]{2,1,0:T(1,128)S(1)}, f32[1...) fusion(f32[18,30,3000]{2,1,0:T(8,128)} %param.8), kind=kLoop, calls=%fused_computation.765 | loop fusion | bytes 8208000 | tf_op jit(solution)/shard_map/slice | solution.py:62
  49.1 6.2 fusion.101
  56.0 6.2 fusion.98
  62.4 20.1 %fusion.206 = (f32[18,3000]{1,0:T(8,128)}, f32[18,3000]{1,0:T(8,128)}, f32[18,3000]{1,0:T(8,128)}, f32[18,3000]{1,0:T(8,128)}, f32[18,3000]{1,0:T(8,128)}, /*ind...) fusion(f32[18,1,3000]{2,1,0:T(1,128)S(1)} %get-tuple-element.25, ...), kind=kLoop, calls=%fused_computation.453 | loop fusion | flops 11070000 | bytes 13122092 | tf_op jit(solution)/shard_map/div | solution.py:83
  83.0 19.4 %fusion.203 = (f32[18,3000]{1,0:T(8,128)}, f32[18,3000]{1,0:T(8,128)}, f32[18,3000]{1,0:T(8,128)}, f32[18,3000]{1,0:T(8,128)}, f32[18,3000]{1,0:T(8,128)}, /*ind...) fusion(pred[18,3000]{1,0:T(8,128)(4,1)S(1)} %get-tuple-element., ...), kind=kLoop, calls=%fused_computation.450 | loop fusion | flops 9990000 | bytes 12906092 | tf_op jit(solution)/shard_map/div | solution.py:82
  102.6 33.1 %select_add_fusion.58 = (f32[18,3000]{1,0:T(8,128)}, f32[18,3000]{1,0:T(8,128)}, f32[18,3000]{1,0:T(8,128)S(1)}, f32[18,3000]{1,0:T(8,128)S(1)}, f32[18,3000]{1,...) fusion(f32[]{:T(128)} %bitcast.57, ...), kind=kLoop, calls=%fused_computation.580 | loop fusion | flops 21492000 | bytes 33804116 | tf_op jit(solution)/shard_map/add | solution.py:102
  171.9 34.4 %stack.371 = f32[18,30,3000]{2,1,0:T(8,128)} concatenate(f32[18,1,3000]{2,1,0:T(1,128)S(1)} %copy-done.89, f32[18,1,3000]{2,1,0:T(1,128)} %copy.368, f32[18,1,3000]{2,1,0:T(1,128)} %copy.369, f32[18,1,3000]{2,1,0:T(1,128)} %copy.370, f32[18,1,3000]{2,1,0:T(1,128)} %copy.371, f32[18,1,3000]{2,1,0:T(1,128)} %copy.372, f32[18,1,3000]{2,1,0:T(1,128)} %copy.373, ...), dimensions={1} | concatenate | bytes 12960000 | tf_op jit(solution)/shard_map/stack | solution.py:104
  206.3 9.1 gather_fusion.1
  216.2 12.4 %select_select_fusion = f32[32,30,3000]{2,1,0:T(8,128)} fusion(f32[32,30,3000]{2,1,0:T(8,128)} %gather_fusion.1, pred[32]{0:T(512)(128)(4,1)S(1)} %copy-done.115, pred[32]{0:T(512)(128)(4,1)S(1)} %copy-done.114), kind=kLoop, calls=%fused_computation.4 | loop fusion | flops 5760000 | bytes 23040064 | tf_op jit(solution)/shard_map/jit(_where)/select_n | solution.py:178
  229.4 6.8 all-to-all-start.1
  254.2 10.5 %copy.402 = f32[18,30,3000]{2,1,0:T(8,128)} copy(f32[18,30,3000]{2,0,1:T(8,128)} %get-tuple-element.284) | data formatting | bytes 12960000
  264.8 6.8 copy.403
  273.6 145.6 %all-to-all-done.1 = f32[32,30,3000]{2,1,0:T(8,128)} async-done(((f32[32,30,3000]{2,1,0:T(8,128)}), f32[32,30,3000]{2,1,0:T(8,128)}, u32[]{:S(2)}, u32[]{:S(2)}) %all-to-all-start.1) | async-done | bytes 11520032 | tf_op jit(solution)/shard_map/all_to_all | solution.py:180
  419.3 8.5 gather_fusion.2
  427.7 14.1 %gather.16 = f32[6,3,30,50,60]{4,3,2,1,0:T(8,128)} reshape(f32[18,30,3000]{2,1,0:T(8,128)} %gather_fusion.2) | data formatting | bytes 12960000 | tf_op jit(solution)/shard_map/jit(_take)/gather | solution.py:184
  441.8 13.4 %select_bitcast_fusion = f32[30,6,50,3,60]{4,2,0,3,1:T(8,128)} fusion(f32[6,3,30,50,60]{4,3,2,1,0:T(8,128)} %gather.16, pred[6,3]{1,0:T(8,128)(4,1)S(1)} %compare_and_fusion, pred[6,3]{1,0:T(8,128)(4,1)S(1)} %broadcast_in_dim.336), kind=kLoop, calls=%fused_computation.3 | loop fusion | flops 3240000 | bytes 12960036 | tf_op jit(solution)/shard_map/transpose | solution.py:117
  455.2 17.3 %copy.396 = f32[30,6,50,3,60]{4,3,2,1,0:T(4,128)} copy(f32[30,6,50,3,60]{4,2,0,3,1:T(8,128)} %select_bitcast_fusion) | data formatting | bytes 12960000 | tf_op jit(solution)/shard_map/transpose | solution.py:117
  472.5 17.7 %reshape.115 = f32[30,300,180]{2,1,0:T(8,128)} reshape(f32[30,6,50,3,60]{4,3,2,1,0:T(4,128)} %copy.396) | data formatting | bytes 12960000 | tf_op jit(solution)/shard_map/reshape | solution.py:118
  507.7 8.8 fusion.301
  523.8 4.8 collective-permute-start.2
  540.0 5.9 fusion.5
  546.7 32.6 %fusion.8 = (f32[300,180]{1,0:T(8,128)S(1)}, f32[300,180]{1,0:T(8,128)S(1)}, f32[300,180]{1,0:T(8,128)}) fusion(f32[30,300,180]{2,1,0:T(8,128)S(1)} %bitcast.710, f32[31,302,1]{2,1,0:T(8,128)S(1)} %copy-done.1, f32[31,1,180]{2,1,0:T(1,128)S(1)} %collective-permute-done.1, f32[31,1,180]{2,1,0:T(1,128)S(1)} %collective-permute-done, ...), kind=kLoop, calls=%fused_computation.19 | loop fusion | flops 35478000 | bytes 8133856 | tf_op jit(solution)/shard_map/reduce_sum | solution.py:198
  591.6 4.8 collective-permute-start.10
  601.5 69.2 %all-reduce = (f32[]{:T(128)}, f32[]{:T(128)}) all-reduce(f32[]{:T(128)} %get-tuple-element.24, f32[]{:T(128)} %get-tuple-element.23), channel_id=1, replica_groups=mesh['gx'=16,'gy'=8] {'gx','gy'}, use_global_device_ids=true, to_apply=%region_10.11 | all-reduce | flops 2 | bytes 16 | tf_op jit(solution)/shard_map/psum | solution.py:139
  672.8 62.5 %psum.44 = f32[]{:T(128)} all-reduce(f32[]{:T(128)} %get-tuple-element.34), channel_id=1, replica_groups=mesh['gx'=16,'gy'=8] {'gx','gy'}, use_global_device_ids=true, to_apply=%region_14.15 | all-reduce | flops 1 | bytes 8 | tf_op jit(solution)/shard_map/psum | solution.py:139
  746.1 4.7 collective-permute-start.18
  756.6 69.2 %psum.45 = f32[]{:T(128)} all-reduce(f32[]{:T(128)} %get-tuple-element.32), channel_id=1, replica_groups=mesh['gx'=16,'gy'=8] {'gx','gy'}, use_global_device_ids=true, to_apply=%region_16.17 | all-reduce | flops 1 | bytes 8 | tf_op jit(solution)/shard_map/psum | solution.py:219
  828.8 62.5 %psum.46 = f32[]{:T(128)} all-reduce(f32[]{:T(128)} %get-tuple-element.29), channel_id=1, replica_groups=mesh['gx'=16,'gy'=8] {'gx','gy'}, use_global_device_ids=true, to_apply=%region_18.19 | all-reduce | flops 1 | bytes 8 | tf_op jit(solution)/shard_map/psum | solution.py:139
  901.9 4.7 collective-permute-start.26
  912.4 69.2 %psum.47 = f32[]{:T(128)} all-reduce(f32[]{:T(128)} %get-tuple-element.27), channel_id=1, replica_groups=mesh['gx'=16,'gy'=8] {'gx','gy'}, use_global_device_ids=true, to_apply=%region_20.21 | all-reduce | flops 1 | bytes 8 | tf_op jit(solution)/shard_map/psum | solution.py:219
  (489 shorter events, 160.8 us)
Async XLA Ops:
  5.0 224.4 %all-to-all-start = ((s32[16,2,1]{1,2,0:T(1,128)}), s32[16,2,1]{1,2,0:T(1,128)S(1)}, u32[]{:S(2)}, u32[]{:S(2)}) async-start(s32[16,2,1]{1,2,0:T(1,128)} %bitcast.151), calls=%async_computation | async-start | bytes 16384 | tf_op jit(solution)/shard_map/all_to_all | solution.py:181
  229.4 189.9 %all-to-all-start.1 = ((f32[32,30,3000]{2,1,0:T(8,128)}), f32[32,30,3000]{2,1,0:T(8,128)}, u32[]{:S(2)}, u32[]{:S(2)}) async-start(f32[32,30,3000]{2,1,0:T(8,128)} %select_select_fusion), calls=%async_computation.1 | async-start | bytes 25165824 | tf_op jit(solution)/shard_map/all_to_all | solution.py:180
  491.5 11.7 %collective-permute-start = (f32[31,1,180]{2,1,0:T(1,128)S(1)}, f32[31,1,180]{2,1,0:T(1,128)S(1)}, u32[]{:S(2)}, u32[]{:S(2)}) collective-permute-start(f32[31,1,180]{2,1,0:T(1,128)S(1)} %get-tuple-element.218), channel_id=1, source_target_pairs={{0,1},{1,2},{2,3},{3,4},{4,5},{5,6},{6,7},{7,0},{8,9},{9,10},{10,1... | collective-permute-start | bytes 66968 | tf_op jit(solution)/shard_map/ppermute | solution.py:32
  495.1 8.1 collective-permute-start.1
  495.1 4.4 collective-permute-start.4
  499.5 8.2 collective-permute-start.5
  507.7 21.0 %collective-permute-start.6 = (f32[31,180]{1,0:T(8,128)S(1)}, f32[31,180]{1,0:T(8,128)S(1)}, u32[]{:S(2)}, u32[]{:S(2)}) collective-permute-start(f32[31,180]{1,0:T(8,128)S(1)} %collective-permute-done.5), channel_id=1, source_target_pairs={{0,32},{8,40},{16,48},{24,56},{32,0},{40,8},{48,16},{56,24},{64,96... | collective-permute-start | bytes 66968 | tf_op jit(solution)/shard_map/ppermute | solution.py:22
  520.1 9.7 collective-permute-start.3
  523.8 9.2 collective-permute-start.2
  528.6 7.4 collective-permute-start.7
  580.7 6.3 collective-permute-start.8
  583.9 3.3 collective-permute-start.9
  586.4 3.9 collective-permute-start.13
  590.3 6.1 collective-permute-start.14
  591.5 9.0 collective-permute-start.11
  591.6 9.0 collective-permute-start.10
  596.4 3.9 collective-permute-start.15
  736.7 5.6 collective-permute-start.16
  738.3 4.0 collective-permute-start.17
  738.3 2.7 collective-permute-start.20
  741.1 3.9 collective-permute-start.21
  745.0 5.8 collective-permute-start.22
  746.0 9.0 collective-permute-start.19
  746.1 8.9 collective-permute-start.18
  750.8 3.9 collective-permute-start.23
  892.7 5.6 collective-permute-start.24
  894.3 4.0 collective-permute-start.25
  897.1 3.9 collective-permute-start.29
  901.0 5.6 collective-permute-start.30
  901.8 9.0 collective-permute-start.27
  901.9 8.9 collective-permute-start.26
  906.6 3.9 collective-permute-start.31
  (128 other events, 2139.3 us)
where the time goes:
time: 995 us; the launch traced here: 986 us
  blocking collectives  333 us (33%)
  local copies, waits for them, and re-layouts  234 us (24%)
  other arithmetic  182 us (18%)
  waiting for transfers between devices  171 us (17%)
  starting transfers between devices  56.9 us (6%)
    psum x3, blocking collectives, global_sum(): return lax.psum(jnp.sum(values), ('gx', 'gy'))  194 us
    all_to_all x1, waiting for transfers between devices, on_device(): lax.all_to_all(send_cols, 'gx', split_axis=0, concat_axis=0, tiled=True)  146 us
    psum x2, blocking collectives, on_device(): lax.psum(jnp.sum(direction * result), ('gx', 'gy'))  138 us
    another operation x31, local copies, waits for them, and re-layouts, weight_balanced(): return jnp.stack(layers_out, axis=1)  60.6 us
    unnamed x318, local copies, waits for them, and re-layouts  45.7 us
    reduce_sum x2, other arithmetic, on_device(): jnp.sum(jnp.where(layer_index < face_levels, neighbour[:-1] - region, 0.0...  38.5 us
    add x1, other arithmetic, weight_balanced(): running = running + mass_per_volume  33.1 us
    slice x2, local copies, waits for them, and re-layouts, thomas_vertical_inverse(): salt_term = saltiness_anomaly[:, stratum_position, :]  26.4 us
  transfers between devices with their start and end apart: 34, of which 11 were waited for; matrix products, arithmetic and copies ran while one was open for 29% of the time, Pallas kernels for 0%

commit v1 on v0

v1 whole, which is shorter than its diff:
```python
import functools

import jax
import jax.numpy as jnp
from jax import lax
from jax.experimental import pallas as pl
from jax.experimental.pallas import tpu as pltpu
from jax.sharding import PartitionSpec as P

SPAN_E = 60
SPAN_N = 50
KX = 3
KY = 6
LEVELS = 30
SLOTS = KX * KY
CELLS = SPAN_E * SPAN_N
ROWS = KY * SPAN_N
COLS = KX * SPAN_E
TILES = 24
HALINE = 0.8
THERMAL = 0.6
DAMPING = 0.05

TOP = 16
PLANE = 328
UROWS = TOP + SPAN_N * 8
BLK = 32
EAST = COLS - 128
MESH = pl.DeviceIdType.MESH
F32 = jnp.float32
I32 = jnp.int32
VMEM = pltpu.VMEM


def iota(shape, dim):
    return lax.broadcasted_iota(I32, shape, dim)


def lroll(x, shift):
    shift = shift % x.shape[1]
    return x if shift == 0 else pltpu.roll(x, shift, 1)


def sroll(x, shift):
    shift = shift % x.shape[0]
    return x if shift == 0 else pltpu.roll(x, shift, 0)


def lreverse(x):
    lane = iota(x.shape, 1)
    bit = 1
    while bit < 128:
        x = jnp.where((lane & bit) != 0, lroll(x, bit), lroll(x, -bit))
        bit *= 2
    return x


def flip_cols(a, b):
    ra, rb = lreverse(b), lreverse(a)
    shift = 256 - COLS
    lane = iota(a.shape, 1)
    xa, xb = lroll(ra, -shift), lroll(rb, -shift)
    return jnp.where(lane < 128 - shift, xa, xb), jnp.where(lane < 128 - shift, xb, xa)


def barrier(peers):
    sem = pltpu.get_barrier_semaphore()
    for peer in peers:
        pl.semaphore_signal(sem, inc=1, device_id=peer, device_id_type=MESH)
    pl.semaphore_wait(sem, len(peers))


def strips_kernel(n, ng, cap, ids_ref, depth_ref, all_ref, tab_ref, pa, pb, msg, edge, got,
                  s1, r1, s2, r2):
    g = lax.axis_index("gx")
    y = lax.axis_index("gy")
    up, down = lax.rem(y + 1, ng), lax.rem(y + ng - 1, ng)
    barrier([(lax.rem(g + k, n), y) for k in range(1, n)] + [(g, up), (g, down)])
    pa[0:ROWS, :] = depth_ref[:, 0:128]
    pb[0:ROWS, 0:EAST] = depth_ref[:, 128:COLS]
    lane = iota((8, 128), 1)
    strips = [[jnp.zeros((8, 128), I32) for _ in range(2)] for _ in range(KX)]
    ns = []
    for i in range(SPAN_N):
        off = SPAN_E * i % 128
        a = pa[pl.ds(i, 8, stride=SPAN_N), :]
        b = pb[pl.ds(i, 8, stride=SPAN_N), :]
        cells = [a, a, jnp.where(lane < 64, b, a)]
        here = (lane == off) | (lane == (off + SPAN_E - 1) % 128)
        for bx in range(KX):
            strips[bx][i // 32] = jnp.where(here, lroll(cells[bx], off - SPAN_E * bx), strips[bx][i // 32])
        if i == 0:
            ns = [lroll(cells[bx], -SPAN_E * bx) for bx in range(KX)]
        if i == SPAN_N - 1:
            ns = [
                jnp.where(lane < SPAN_E, ns[bx], lroll(cells[bx], SPAN_E - SPAN_E * bx))
                for bx in range(KX)
            ]
    for bx in range(KX):
        for part, value in enumerate((strips[bx][0], strips[bx][1], ns[bx])):
            msg[pl.ds(bx * 3 + part, 8, stride=9), :] = value
    edge[...] = jnp.zeros((8, 128), I32)
    for bx in range(KX):
        edge[bx : bx + 1, :] = ns[bx][0:1]
        edge[3 + bx : 4 + bx, :] = ns[bx][KY - 1 : KY]
    copies = []
    for slot, target in ((0, up), (1, down)):
        copy = pltpu.make_async_remote_copy(
            edge, got.at[slot], s1.at[slot], r1.at[slot], device_id=(g, target), device_id_type=MESH
        )
        copy.start()
        copies.append(copy)
    row = iota((1, 128), 1)
    code = jnp.full((1, 128), -1, I32)
    owners = []
    for s in range(SLOTS):
        block = jnp.maximum(ids_ref[s], 0)
        bx = lax.rem(block, KX * n)
        by = lax.rem(lax.div(block, KX * n), KY)
        owner = jnp.where(ids_ref[s] >= 0, lax.div(bx, KX), -1)
        rank = jnp.int32(0)
        for other in owners:
            rank = rank + jnp.where(other == owner, 1, 0)
        owners.append(owner)
        value = (owner * 32 + by * KX + lax.rem(bx, KX)) * 32 + rank
        code = jnp.where(row == s, jnp.where(owner >= 0, value, -1), code)
    msg[54:55, :] = code
    for bx, place in enumerate((55, 62, 63)):
        msg[place : place + 1, :] = lroll(lreverse(ns[bx]), -8)[KY - 1 : KY]
    for copy in copies:
        copy.wait()
    msg[56:59, :] = got[1][0:3]
    msg[59:62, :] = got[0][3:6]
    copies = []
    for k in range(1, n):
        target = lax.rem(g + k, n)
        copy = pltpu.make_async_remote_copy(
            msg.at[pl.ds(0, 64)], all_ref.at[g], s2.at[k], r2.at[k], device_id=(target, y), device_id_type=MESH
        )
        copy.start()
        copies.append(copy)
    all_ref[pl.ds(g, 1)] = msg[0:64, :][None]
    for copy in copies:
        copy.wait()
    codes = all_ref[:, 54, :]
    key = codes >> 5
    rank = codes & 31
    source = iota((n, 128), 0)
    number = (source * cap + rank + 1).astype(F32)
    for p in range(SLOTS):
        hit = jnp.where(key == g * 32 + p, number, 0.0)
        hit = jnp.sum(jnp.sum(hit, axis=0, keepdims=True), axis=1, keepdims=True)
        tab_ref[p : p + 1, :] = jnp.broadcast_to(hit.astype(I32) - 1, (1, 128))
    tab_ref[SLOTS:24, :] = jnp.full((24 - SLOTS, 128), -1, I32)


def ahead(x, step):
    a = lroll(x, -step)
    return jnp.where(iota(x.shape, 1) < 128 - step, a, sroll(a, -1))


def behind(x, step):
    a = lroll(x, step)
    return jnp.where(iota(x.shape, 1) >= step, a, sroll(a, 1))


def columns_kernel(n, ng, cap, ids_ref, dfac_ref, flux_ref, depth_ref, strips_ref, heat_ref, salt_ref,
                   heat_out, salt_out, msg_ref, nflat, fflat, coef, jcol, inh, ins, yh, ys, oh, os_, count):
    step = pl.program_id(0)
    shape = (TILES, 128)
    row24 = iota(shape, 0)
    lane24 = iota(shape, 1)
    cell = row24 * 128 + lane24
    lane = iota((1, 128), 1)
    last = CELLS - 128 * (TILES - 1)

    @pl.when(step == 0)
    def _():
        for t in range(TILES):
            width = 128 if t < TILES - 1 else last
            cols = slice(t * 128, t * 128 + width)
            for first in (0, 8, 16):
                rows = min(8, SLOTS - first)
                place = pl.ds(first * TILES + t, rows, stride=TILES)
                d = depth_ref[first : first + rows, cols]
                f = flux_ref[first : first + rows, cols]
                if width < 128:
                    d = jnp.concatenate([d, jnp.zeros((rows, 128 - width), I32)], axis=1)
                    f = jnp.concatenate([f, jnp.zeros((rows, 128 - width), F32)], axis=1)
                nflat[place, :] = d
                fflat[place, :] = f
        gain = jnp.zeros((1, 128), F32)
        for k in range(LEVELS):
            above = dfac_ref[k - 1] if k > 0 else jnp.float32(0)
            below = dfac_ref[k] if k + 1 < LEVELS else jnp.float32(0)
            base = (1.0 + above) - above * gain
            full = 1.0 / (base + below)
            gain = below * full
            coef[0, k : k + 1, :] = full
            coef[1, k : k + 1, :] = 1.0 / base
            coef[2, k : k + 1, :] = jnp.broadcast_to(above, (1, 128))
            coef[3, k : k + 1, :] = gain
        owner = cell.astype(F32)
        whole = jnp.floor((owner + 0.5) * (1.0 / SPAN_E))
        jcol[...] = cell - whole.astype(I32) * SPAN_E
        for d in range(n):
            count[d] = 0

    for t in range(TILES):
        width = 128 if t < TILES - 1 else last
        cols = slice(t * 128, t * 128 + width)
        inh[t * 32 : t * 32 + LEVELS, 0:width] = heat_ref[0, :, cols]
        ins[t * 32 : t * 32 + LEVELS, 0:width] = salt_ref[0, :, cols]

    mine = pl.ds(pl.multiple_of(step * TILES, 8), TILES)
    depth = nflat[mine, :]
    wet = depth > 0
    h = s = None
    for k in range(LEVELS):
        level = pl.ds(k, TILES, stride=32)
        rh = inh[level, :]
        rs = ins[level, :]
        deeper = depth > k + 1
        if k == 0:
            rh = rh + jnp.where(wet, fflat[mine, :], 0.0)
            pivot = jnp.where(deeper, coef[0, 0:1, :], 1.0)
            h = rh * pivot
            s = rs * pivot
        else:
            above = jnp.where(wet, coef[2, k : k + 1, :], 0.0)
            pivot = jnp.where(wet, coef[1, k : k + 1, :], 1.0)
            if k + 1 < LEVELS:
                pivot = jnp.where(deeper, coef[0, k : k + 1, :], pivot)
            h = (rh + above * h) * pivot
            s = (rs + above * s) * pivot
        if k + 1 < LEVELS:
            yh[k * TILES : (k + 1) * TILES, :] = h
            ys[k * TILES : (k + 1) * TILES, :] = s
        wet = deeper
    level = pl.ds(LEVELS - 1, TILES, stride=32)
    oh[level, :] = h
    os_[level, :] = s
    for k in range(LEVELS - 2, -1, -1):
        gain = jnp.where(depth > k + 1, coef[3, k : k + 1, :], 0.0)
        h = yh[k * TILES : (k + 1) * TILES, :] + gain * h
        s = ys[k * TILES : (k + 1) * TILES, :] + gain * s
        level = pl.ds(k, TILES, stride=32)
        oh[level, :] = h
        os_[level, :] = s
    for t in range(TILES):
        width = 128 if t < TILES - 1 else last
        cols = slice(t * 128, t * 128 + width)
        heat_out[0, :, cols] = oh[t * 32 : t * 32 + LEVELS, 0:width]
        salt_out[0, :, cols] = os_[t * 32 : t * 32 + LEVELS, 0:width]

    blocks_x = KX * n
    ident = ids_ref[step]
    block = jnp.maximum(ident, 0)
    bx = lax.rem(block, blocks_x)
    by = lax.div(block, blocks_x)
    byl = lax.rem(by, KY)
    dev = lax.div(bx, KX)
    bxl = lax.rem(bx, KX)

    def strip(device, place):
        return strips_ref[device, pl.ds(place, 1), :]

    def sides(col, part):
        return strip(lax.div(col, KX), (byl * KX + lax.rem(col, KX)) * 3 + part)

    east = lax.rem(bx + 1, blocks_x)
    west = lax.rem(bx + blocks_x - 1, blocks_x)
    ew = [
        jnp.where((lane & 3) == 3, lroll(sides(east, part), SPAN_E - 1), lroll(sides(west, part), 1 - SPAN_E))
        for part in range(2)
    ]
    ew = jnp.where(row24 < 15, ew[0], ew[1])
    mirror = blocks_x - 1 - bx
    mirrored = lax.rem(mirror, KX)
    folded = by == KY * ng - 1
    inner = byl < KY - 1
    north_dev = jnp.where(folded, lax.div(mirror, KX), dev)
    north_row = jnp.where(
        inner,
        ((byl + 1) * KX + bxl) * 3 + 2,
        jnp.where(folded, jnp.where(mirrored == 0, 55, 61 + mirrored), 56 + bxl),
    )
    north = lroll(strip(north_dev, north_row), -4)
    south_row = jnp.where(byl > 0, ((byl - 1) * KX + bxl) * 3 + 2, 59 + bxl)
    south = jnp.where(by > 0, lroll(strip(dev, south_row), -SPAN_E), 0)
    j = jcol[...]
    inside = cell < CELLS
    first_j = j == 0
    last_j = j == SPAN_E - 1
    first_i = cell < SPAN_E
    last_i = cell >= CELLS - SPAN_E
    faces = (
        jnp.minimum(depth, jnp.where(last_j, ew, ahead(depth, 1))),
        jnp.minimum(depth, jnp.where(first_j, ew, behind(depth, 1))),
        jnp.minimum(depth, jnp.where(last_i, north, ahead(depth, SPAN_E))),
        jnp.minimum(depth, jnp.where(first_i, south, behind(depth, SPAN_E))),
    )
    sums = [jnp.zeros(shape, F32) for _ in range(4)]
    pressure = jnp.zeros(shape, F32)
    total = jnp.zeros(shape, F32)
    for k in range(LEVELS):
        level = pl.ds(k, TILES, stride=32)
        pressure = pressure + (HALINE * os_[level, :] - THERMAL * oh[level, :])
        total = total + pressure
        sums = [jnp.where(face == k + 1, total, held) for face, held in zip(faces, sums)]
    sums = [jnp.where(inside, held, 0.0) for held in sums]
    se, sw, sn, ss = sums
    local = jnp.where(last_j, 0.0, ahead(sw, 1)) - se
    local = local + (jnp.where(first_j, 0.0, behind(se, 1)) - sw)
    local = local + (jnp.where(last_i, 0.0, ahead(ss, SPAN_E)) - sn)
    local = local + (jnp.where(first_i, 0.0, behind(sn, SPAN_E)) - ss)
    local = jnp.where(inside, local, 0.0)
    rim = jnp.where(last_j, se, jnp.where(first_j, sw, 0.0))
    rim0 = jnp.sum(jnp.where(row24 < 15, rim, 0.0), axis=0, keepdims=True)
    rim1 = jnp.sum(jnp.where(row24 >= 15, rim, 0.0), axis=0, keepdims=True)
    top = jnp.sum(jnp.where(last_i, sn, 0.0), axis=0, keepdims=True)
    bottom = jnp.sum(jnp.where(first_i, ss, 0.0), axis=0, keepdims=True)
    cap_row = jnp.where(lane < SPAN_E, bottom, jnp.where(lane < 2 * SPAN_E, lroll(top, 64), 0.0))

    @pl.when(ident >= 0)
    def _():
        rank = count[dev]
        count[dev] = rank + 1
        msg_ref[dev, pl.ds(pl.multiple_of(rank * TILES, 8), TILES), :] = local
        base = cap * TILES + rank * 3
        for part, value in enumerate((rim0, rim1, cap_row)):
            msg_ref[dev, pl.ds(base + part, 1), :] = value


def barotropic_kernel(n, ng, cap, tab_ref, depth_ref, msg_ref, height_ref, misfit_ref,
                      recv, blk, dpl, upl, zpl, wts, qpl, row_out, row_in, col_out, col_in,
                      red_out, red_x, red_y, own_sem, a2a_s, a2a_r, row_s, row_r, col_s, col_r,
                      rx_s, rx_r, ry_s, ry_r):
    g = lax.axis_index("gx")
    y = lax.axis_index("gy")
    band = [(lax.rem(g + k, n), y) for k in range(1, n)]
    column = [(g, lax.rem(y + k, ng)) for k in range(1, ng)]
    barrier(band + column)
    own = pltpu.make_async_copy(msg_ref.at[g], recv.at[g], own_sem)
    own.start()
    sends = []
    for k, peer in enumerate(band):
        copy = pltpu.make_async_remote_copy(
            msg_ref.at[peer[0]], recv.at[g], a2a_s.at[k], a2a_r.at[k], device_id=peer, device_id_type=MESH
        )
        copy.start()
        sends.append(copy)

    lane = iota((8, 128), 1)
    sub = iota((8, 128), 0)
    at_top = lax.div(y + 1, ng)
    is_top = y == ng - 1
    has_south = y > 0

    def rows_start(k, north, north_folded, south):
        flipped = flip_cols(*north_folded)
        for half in range(2):
            row_out[k, 0, half] = jnp.where(is_top, flipped[half], north[half])
            row_out[k, 1, half] = south[half]
        up = pltpu.make_async_remote_copy(
            row_out.at[k, 0], row_in.at[k, at_top], row_s.at[k, 0], row_r.at[k, at_top],
            device_id=(g + at_top * (n - 1 - 2 * g), y + 1 - at_top), device_id_type=MESH,
        )
        down = pltpu.make_async_remote_copy(
            row_out.at[k, 1], row_in.at[k, 1], row_s.at[k, 1], row_r.at[k, 1],
            device_id=(g, lax.rem(y + ng - 1, ng)), device_id_type=MESH,
        )
        up.start()

        @pl.when(has_south)
        def _():
            down.start()

        return up, down

    def rows_wait(k, up, down):
        up.wait_send()

        @pl.when(has_south)
        def _():
            down.wait_send()
            south = pltpu.make_async_remote_copy(
                row_out.at[k, 1], row_in.at[k, 0], row_s.at[k, 1], row_r.at[k, 0],
                device_id=(g, lax.rem(y + ng - 1, ng)), device_id_type=MESH,
            )
            south.wait_recv()

        down.wait_recv()

        @pl.when(jnp.logical_not(has_south))
        def _():
            row_in[k, 0] = jnp.zeros((2, 8, 128), F32)

        return [row_in[k, 0, half] for half in range(2)], [row_in[k, 1, half] for half in range(2)]

    def cols_start(k):
        copies = []
        for slot, target in ((0, lax.rem(g + 1, n)), (1, lax.rem(g + n - 1, n))):
            copy = pltpu.make_async_remote_copy(
                col_out.at[k, slot], col_in.at[k, slot], col_s.at[k, slot], col_r.at[k, slot],
                device_id=(target, y), device_id_type=MESH,
            )
            copy.start()
            copies.append(copy)
        return copies

    def halo(k, plane):
        north = [plane[half, 312:320, :] for half in range(2)]
        south = [plane[half, 16:24, :] for half in range(2)]
        turned = [
            jnp.where(sub == 0, sroll(v, -3), jnp.where(sub == 1, sroll(v, -1), sroll(v, 1))) for v in north
        ]
        below, above = rows_wait(k, *rows_start(k, north, turned, south))
        for half in range(2):
            plane[half, 8:16, :] = sroll(below[half], 4)
            plane[half, 312:320, :] = jnp.where(sub < 4, north[half], sroll(above[half], 4))
        to_east = jnp.zeros((8, 128), F32)
        to_west = jnp.zeros((8, 128), F32)
        for t in range(39):
            here = (lane >= 3 * t) & (lane < 3 * t + 3)
            rows = slice(8 + 8 * t, 16 + 8 * t)
            to_east = jnp.where(here, lroll(plane[1, rows, :], 3 * t - (EAST - 3)), to_east)
            to_west = jnp.where(here, lroll(plane[0, rows, :], 3 * t), to_west)
        col_out[k, 0, 0:8, :] = to_east
        col_out[k, 1, 0:8, :] = to_west
        for copy in cols_start(k):
            copy.wait()
        from_west = col_in[k, 0, 0:8, :]
        from_east = col_in[k, 1, 0:8, :]
        for t in range(39):
            rows = slice(8 + 8 * t, 16 + 8 * t)
            plane[1, rows, :] = jnp.where(
                lane >= 125,
                lroll(from_west, 125 - 3 * t),
                jnp.where((lane >= EAST) & (lane < EAST + 3), lroll(from_east, EAST - 3 * t), plane[1, rows, :]),
            )

    zero8 = jnp.zeros((8, 128), F32)
    for half in range(2):
        dpl[half, 0:16, :] = jnp.zeros((16, 128), F32)
        dpl[half, 312:PLANE, :] = jnp.zeros((PLANE - 312, 128), F32)
    dpl[0, TOP : TOP + ROWS, :] = depth_ref[:, 0:128].astype(F32)
    dpl[1, TOP : TOP + ROWS, :] = jnp.zeros((ROWS, 128), F32)
    dpl[1, TOP : TOP + ROWS, 0:EAST] = depth_ref[:, 128:COLS].astype(F32)
    for half in range(2):
        for ref in (zpl, qpl.at[0], qpl.at[1], qpl.at[2], qpl.at[3]):
            ref[half, 0:8, :] = zero8
            ref[half, 320:PLANE, :] = zero8
    halo(0, dpl)

    span = 24
    chunks = 13
    lane_c = iota((span, 128), 1)

    def rows_at(t, shift=0):
        return pl.ds(8 + t * span + shift, span)

    def both(ref, rows):
        return [ref[half, rows, :] for half in range(2)]

    def from_east(pair):
        a, b = [lroll(v, -1) for v in pair]
        return jnp.where(lane_c < 127, a, b), jnp.where(lane_c < 127, b, a)

    def from_west(pair):
        a, b = [lroll(v, 1) for v in pair]
        return jnp.where(lane_c >= 1, a, b), jnp.where(lane_c >= 1, b, a)

    def weigh(t, carry):
        rows = rows_at(t)
        d = both(dpl, rows)
        beside = (from_east(d), from_west(d), both(dpl, rows_at(t, 1)), both(dpl, rows_at(t, -1)))
        r = iota((span, 128), 0) + (8 + t * span)
        for half in range(2):
            damp = jnp.where(d[half] > 0, DAMPING, 1.0)
            diagonal = damp
            for side in range(4):
                w = jnp.minimum(d[half], beside[side][half]) * (1.0 / LEVELS)
                wts[side, half, rows, :] = w
                diagonal = diagonal + w
            inverse = 1.0 / diagonal
            wts[4, half, rows, :] = damp
            wts[5, half, rows, :] = inverse
            inside = (r >= TOP) & (r < TOP + ROWS)
            if half == 1:
                inside = inside & (lane_c < EAST)
            wts[6, half, rows, :] = jnp.where(inside, inverse, 0.0)
        return carry

    lax.fori_loop(0, chunks, weigh, 0)

    own.wait()
    for copy in sends:
        copy.wait()
    for bx in range(KX):
        blk[(bx * 8 + KY) * BLK : (bx + 1) * 8 * BLK, :] = jnp.zeros((2 * BLK, 128), F32)
        wanted = [
            jnp.broadcast_to(tab_ref[by * KX + bx : by * KX + bx + 1, :], (8, 128)) for by in range(KY)
        ]

        def pick(source, held, wanted=wanted):
            held = list(held)
            for rank in range(cap):
                parts = [recv[source, rank * TILES + 8 * v : rank * TILES + 8 * v + 8, :] for v in range(3)]
                first = cap * TILES + rank * 3
                rest = recv[source, first : first + 3, :]
                for by in range(KY):
                    hit = wanted[by] == source * cap + rank
                    for v in range(3):
                        held[by * 4 + v] = jnp.where(hit, parts[v], held[by * 4 + v])
                    held[by * 4 + 3] = jnp.where(hit[0:3], rest, held[by * 4 + 3])
            return tuple(held)

        start = ([zero8] * 3 + [jnp.zeros((3, 128), F32)]) * KY
        held = lax.fori_loop(0, n, pick, tuple(start))
        for by in range(KY):
            base = (bx * 8 + by) * BLK
            for v in range(3):
                blk[base + 8 * v : base + 8 * v + 8, :] = held[by * 4 + v]
            blk[base + TILES : base + TILES + 3, :] = held[by * 4 + 3]

    def rows_of(bx, row):
        return blk[pl.ds(bx * 8 * BLK + row, 8, stride=BLK), :]

    rims = [[rows_of(bx, TILES + part) for part in range(2)] for bx in range(KX)]
    for part in range(2):
        col_out[1, 0, 8 * part : 8 * part + 8, :] = rims[KX - 1][part]
        col_out[1, 1, 8 * part : 8 * part + 8, :] = rims[0][part]
    cap_rows = [rows_of(bx, TILES + 2) for bx in range(KX)]

    def lay(v):
        tail = jnp.where(lane < EAST, v[2], 0.0)
        return jnp.where(lane < 60, v[0], jnp.where(lane < 120, v[1], v[2])), tail

    souths = lay([lroll(cap_rows[bx], SPAN_E * bx) for bx in range(KX)])
    norths = lay([lroll(cap_rows[bx], SPAN_E * bx - SPAN_E) for bx in range(KX)])
    waits = rows_start(1, norths, [sroll(v, 8 - (KY - 1)) for v in norths], souths)
    col_copies = cols_start(1)
    for i in range(SPAN_N):
        t, off = SPAN_E * i // 128, SPAN_E * i % 128
        cells = []
        for bx in range(KX):
            value = rows_of(bx, t)
            if off + SPAN_E > 128:
                value = jnp.where(lane >= off, value, rows_of(bx, t + 1))
            cells.append(lroll(value, SPAN_E * bx - off))
        first, second = lay(cells)
        rim = [rims[bx][i // 32] for bx in range(KX)]
        first = first + jnp.where(
            lane == 59,
            lroll(rim[1], 59 - off),
            jnp.where(
                lane == 60,
                lroll(rim[0], 1 - off),
                jnp.where(lane == 119, lroll(rim[2], 119 - off), jnp.where(lane == 120, lroll(rim[1], 61 - off), 0.0)),
            ),
        )
        if i == SPAN_N - 1:
            first = first + jnp.where(sub < KY - 1, sroll(souths[0], -1), 0.0)
            second = second + jnp.where(sub < KY - 1, sroll(souths[1], -1), 0.0)
        if i == 0:
            first = first + jnp.where((sub > 0) & (sub < KY), sroll(norths[0], 1), 0.0)
            second = second + jnp.where((sub > 0) & (sub < KY), sroll(norths[1], 1), 0.0)
        upl[0, pl.ds(TOP + i, 8, stride=SPAN_N), :] = first
        upl[1, pl.ds(TOP + i, 8, stride=SPAN_N), :] = second
    below, above = rows_wait(1, *waits)
    for copy in col_copies:
        copy.wait()
    for half in range(2):
        upl[half, TOP : TOP + 1, :] = upl[half, TOP : TOP + 1, :] + below[half][KY - 1 : KY]
        end = TOP + ROWS - 1
        upl[half, end : end + 1, :] = upl[half, end : end + 1, :] + above[half][0:1]
        upl[half, 8:16, :] = zero8
    for i in range(SPAN_N):
        off = SPAN_E * i % 128
        part = slice(8 * (i // 32), 8 * (i // 32) + 8)
        rows = pl.ds(TOP + i, 8, stride=SPAN_N)
        west = lroll(col_in[1, 0, part, :], 1 - SPAN_E - off)
        east = lroll(col_in[1, 1, part, :], COLS - 1 - off)
        good = sub < KY
        upl[0, rows, :] = upl[0, rows, :] + jnp.where((lane == 0) & good, west, 0.0)
        upl[1, rows, :] = upl[1, rows, :] + jnp.where((lane == EAST - 1) & good, east, 0.0)

    def begin(t, carry):
        rows = rows_at(t)
        for half in range(2):
            rhs = upl[half, rows, :] * (1.0 / LEVELS)
            qpl[0, half, rows, :] = rhs
            zpl[half, rows, :] = rhs * wts[5, half, rows, :]
        return carry

    lax.fori_loop(0, chunks, begin, 0)
    halo(2, zpl)

    def image(out, scale_next):
        def body(t, carry):
            rows = rows_at(t)
            v = both(zpl, rows)
            beside = (from_east(v), from_west(v), both(zpl, rows_at(t, 1)), both(zpl, rows_at(t, -1)))
            for half in range(2):
                result = wts[4, half, rows, :] * v[half]
                for side in range(4):
                    result = result + wts[side, half, rows, :] * (v[half] - beside[side][half])
                qpl[out, half, rows, :] = result
            return carry

        lax.fori_loop(0, chunks, body, 0)
        if scale_next:

            def scale(t, carry):
                rows = rows_at(t)
                for half in range(2):
                    zpl[half, rows, :] = qpl[out, half, rows, :] * wts[5, half, rows, :]
                return carry

            lax.fori_loop(0, chunks, scale, 0)

    def everywhere(k, parts):
        red_out[k, 0] = zero8
        for place, part in enumerate(parts):
            red_out[k, 0, place : place + 1, :] = jnp.sum(part, axis=0, keepdims=True)
        for level, (peers, into, sem_s, sem_r, me) in enumerate(
            ((band, red_x, rx_s, rx_r, g), (column, red_y, ry_s, ry_r, y))
        ):
            copies = []
            for number, peer in enumerate(peers):
                copy = pltpu.make_async_remote_copy(
                    red_out.at[k, level], into.at[k, me], sem_s.at[k, number], sem_r.at[k, number],
                    device_id=peer, device_id_type=MESH,
                )
                copy.start()
                copies.append(copy)
            into[k, pl.ds(me, 1)] = red_out[k, level][None]
            for copy in copies:
                copy.wait()
            total = jnp.sum(into[k], axis=0)
            if level == 0:
                red_out[k, 1] = total
        total = jnp.sum(total, axis=1, keepdims=True)
        return [jnp.broadcast_to(total[place : place + 1], (8, 128)) for place in range(len(parts))]

    image(1, True)

    def first_dots(t, carry):
        rows = rows_at(t)
        a, b = carry
        for half in range(2):
            z = qpl[0, half, rows, :] * wts[6, half, rows, :]
            a = a + qpl[0, half, rows, :] * z
            b = b + qpl[1, half, rows, :] * z
        return a, b

    zero_c = jnp.zeros((span, 128), F32)
    mu = everywhere(0, lax.fori_loop(0, chunks, first_dots, (zero_c, zero_c)))
    image(2, True)
    image(3, False)
    norm = mu[0]
    ray = mu[1] / norm
    ray_c = jnp.broadcast_to(ray[0:1], (span, 128))

    def shift(t, carry):
        rows = rows_at(t)
        c = list(carry)
        for half in range(2):
            w0, w1, w2, w3 = [qpl[j, half, rows, :] for j in range(4)]
            q1 = w1 - ray_c * w0
            t2 = w2 - ray_c * w1
            t3 = (w3 - ray_c * w2) - ray_c * t2
            q2 = t2 - ray_c * q1
            q3 = t3 - ray_c * q2
            qpl[1, half, rows, :] = q1
            qpl[2, half, rows, :] = q2
            qpl[3, half, rows, :] = q3
            inverse = wts[6, half, rows, :]
            z1 = q1 * inverse
            z2 = q2 * inverse
            c[0] = c[0] + w0 * z1
            c[1] = c[1] + q1 * z1
            c[2] = c[2] + q2 * z1
            c[3] = c[3] + q2 * z2
            c[4] = c[4] + q3 * z2
        return tuple(c)

    moment = everywhere(1, lax.fori_loop(0, chunks, shift, (zero_c,) * 5))
    one = jnp.ones((8, 128), F32)
    scale = one / norm
    c = [one] + [m * scale for m in moment]
    zero = zero8
    rho = [one, zero, zero, zero]
    pi = [one, zero, zero]
    xs = [zero, zero, zero]
    gamma = one
    for it in range(3):
        curve = zero
        for i in range(it + 1):
            for j in range(it + 1):
                curve = curve + (pi[i] * pi[j]) * (ray * c[i + j] + c[i + j + 1])
        alpha = gamma / curve
        xs = [xs[i] + alpha * pi[i] if i <= it else xs[i] for i in range(3)]
        for i in range(it + 2):
            step = ray * pi[i] if i <= it else zero
            if i > 0:
                step = step + pi[i - 1]
            rho[i] = rho[i] - alpha * step
        if it == 2:
            break
        gamma_new = zero
        for i in range(it + 2):
            for j in range(it + 2):
                gamma_new = gamma_new + (rho[i] * rho[j]) * c[i + j]
        beta = gamma_new / gamma
        pi = [rho[i] + beta * pi[i] for i in range(3)]
        gamma = gamma_new

    def finish(first, size):
        rows = pl.ds(TOP + first, size)
        out = pl.ds(first, size)
        x = [jnp.broadcast_to(v[0:1], (size, 128)) for v in xs]
        r = [jnp.broadcast_to(v[0:1], (size, 128)) for v in rho]
        for half in range(2):
            q = [qpl[j, half, rows, :] for j in range(4)]
            high = (x[0] * q[0] + x[1] * q[1] + x[2] * q[2]) * wts[5, half, rows, :]
            rest = r[0] * q[0] + r[1] * q[1] + r[2] * q[2] + r[3] * q[3]
            if half == 0:
                height_ref[out, 0:128] = high
                misfit_ref[out, 0:128] = rest
            else:
                height_ref[out, 128:COLS] = high[:, 0:EAST]
                misfit_ref[out, 128:COLS] = rest[:, 0:EAST]

    def finish_chunk(t, carry):
        finish(pl.multiple_of(t * span, 8), span)
        return carry

    lax.fori_loop(0, ROWS // span, finish_chunk, 0)
    finish(ROWS // span * span, ROWS % span)


def on_device(n, ng, heat, salt, flux, dfac, ids, slot_depth, grid_depth):
    cap = (SLOTS + n - 1) // n
    msg_rows = cap * TILES + (cap * 3 + 7) // 8 * 8
    vmem = pl.BlockSpec(memory_space=VMEM)
    smem = pl.BlockSpec(memory_space=pltpu.SMEM)
    dma = pltpu.SemaphoreType.DMA
    big = 56 * 2**20
    strips, table = pl.pallas_call(
        functools.partial(strips_kernel, n, ng, cap),
        out_shape=(jax.ShapeDtypeStruct((n, 64, 128), I32), jax.ShapeDtypeStruct((24, 128), I32)),
        in_specs=[smem, vmem],
        out_specs=(vmem, vmem),
        scratch_shapes=[
            VMEM((400, 128), I32), VMEM((400, 128), I32), VMEM((72, 128), I32), VMEM((8, 128), I32),
            VMEM((2, 8, 128), I32), dma((2,)), dma((2,)), dma((n,)), dma((n,)),
        ],
        compiler_params=pltpu.CompilerParams(collective_id=0, has_side_effects=True, vmem_limit_bytes=big),
        name="strips",
    )(ids, grid_depth)

    whole = lambda s: (0, 0)
    block = pl.BlockSpec((1, LEVELS, CELLS), lambda s: (s, 0, 0))
    heat_new, salt_new, msg = pl.pallas_call(
        functools.partial(columns_kernel, n, ng, cap),
        grid=(SLOTS,),
        out_shape=(
            jax.ShapeDtypeStruct(heat.shape, F32),
            jax.ShapeDtypeStruct(salt.shape, F32),
            jax.ShapeDtypeStruct((n, msg_rows, 128), F32),
        ),
        in_specs=[
            smem, smem,
            pl.BlockSpec((SLOTS, CELLS), whole),
            pl.BlockSpec((SLOTS, CELLS), whole),
            pl.BlockSpec((n, 64, 128), lambda s: (0, 0, 0)),
            block, block,
        ],
        out_specs=(block, block, pl.BlockSpec((n, msg_rows, 128), lambda s: (0, 0, 0))),
        scratch_shapes=[
            VMEM((SLOTS * TILES, 128), I32), VMEM((SLOTS * TILES, 128), F32), VMEM((4, 32, 128), F32),
            VMEM((TILES, 128), I32),
            VMEM((TILES * 32, 128), F32), VMEM((TILES * 32, 128), F32),
            VMEM((TILES * LEVELS, 128), F32), VMEM((TILES * LEVELS, 128), F32),
            VMEM((TILES * 32, 128), F32), VMEM((TILES * 32, 128), F32),
            pltpu.SMEM((n,), I32),
        ],
        compiler_params=pltpu.CompilerParams(vmem_limit_bytes=big),
        name="columns",
    )(ids, dfac, flux, slot_depth, strips, heat, salt)

    field = jax.ShapeDtypeStruct((ROWS, COLS), F32)
    plane = (2, PLANE, 128)
    height, misfit = pl.pallas_call(
        functools.partial(barotropic_kernel, n, ng, cap),
        out_shape=(field, field),
        in_specs=[vmem, vmem, pl.BlockSpec(memory_space=pl.ANY)],
        out_specs=(vmem, vmem),
        scratch_shapes=[
            VMEM((n, msg_rows, 128), F32), VMEM((KX * 8 * BLK, 128), F32),
            VMEM(plane, F32), VMEM((2, UROWS, 128), F32), VMEM(plane, F32),
            VMEM((7,) + plane, F32), VMEM((4,) + plane, F32),
            VMEM((3, 2, 2, 8, 128), F32), VMEM((3, 2, 2, 8, 128), F32),
            VMEM((3, 2, 16, 128), F32), VMEM((3, 2, 16, 128), F32),
            VMEM((2, 2, 8, 128), F32), VMEM((2, n, 8, 128), F32), VMEM((2, ng, 8, 128), F32),
            dma, dma((n,)), dma((n,)), dma((3, 2)), dma((3, 2)), dma((3, 2)), dma((3, 2)),
            dma((2, n)), dma((2, n)), dma((2, ng)), dma((2, ng)),
        ],
        compiler_params=pltpu.CompilerParams(collective_id=1, has_side_effects=True, vmem_limit_bytes=big),
        name="barotropic",
    )(table, grid_depth, msg)
    return heat_new, salt_new, height, misfit


def solution(mesh):
    n, ng = mesh.shape["gx"], mesh.shape["gy"]
    slots = P(("gx", "gy"), None)
    cube = P(("gx", "gy"), None, None)
    grid = P("gy", "gx")
    return jax.shard_map(
        functools.partial(on_device, n, ng),
        mesh=mesh,
        in_specs=(cube, cube, slots, P(), P(("gx", "gy")), slots, grid),
        out_specs=(cube, cube, grid, grid),
        check_vma=False,
    )
```

time: 995 us -> 116 us (0.12)
  blocking collectives: 333 us -> 0 us
  local copies, waits for them, and re-layouts: 234 us -> 5.47 us
  other arithmetic: 182 us -> 0 us
  waiting for transfers between devices: 171 us -> 0 us
  Pallas kernels: 0 us -> 109 us
  starting transfers between devices: 56.9 us -> 0 us
    psum x5 -> x0, blocking collectives: 333 us -> none  [the longest x3 194 us: global_sum(): return lax.psum(jnp.sum(values), ('gx', 'gy'))]
    all_to_all x2 -> x0, waiting for transfers between devices: 146 us -> none  [the longest x1 146 us: on_device(): lax.all_to_all(send_cols, 'gx', split_axis=0, concat_axis=0, tiled=True)]
    pallas_call x0 -> x3, Pallas kernels: none -> 109 us  [the longest x1 52.6 us: on_device(): pl.pallas_call(functools.partial(barotropic_kernel, n, ng, cap), out_shap...]
    another operation x31 -> x0, local copies, waits for them, and re-layouts: 60.6 us -> none  [weight_balanced(): return jnp.stack(layers_out, axis=1)]
    div x5 -> x0, other arithmetic: 53.3 us -> none  [the longest x2 26.3 us: thomas_vertical_inverse(): salt_rows.append(salt_term / pivots)]
    slice x21 -> x0, local copies, waits for them, and re-layouts: 52.3 us -> none  [the longest x2 26.4 us: thomas_vertical_inverse(): salt_term = saltiness_anomaly[:, stratum_position, :]]
    reduce_sum x10 -> x0, other arithmetic: 45.6 us -> none  [the longest x2 38.5 us: on_device(): jnp.sum(jnp.where(layer_index < face_levels, neighbour[:-1] - region, 0.0...]
    ppermute x32 -> x0, starting transfers between devices: 41.6 us -> none  [the longest x8 19 us: with_halo(): lax.ppermute(head, axis, [((i + 1) % count, i) for i in range(count)])]
  transfers between devices with their start and end apart: 34 -> 0, of which waited for: 11 -> 0; matrix products, arithmetic and copies ran while one was open for 29% -> 0% of each run, Pallas kernels for 0% -> 0%
where the time goes in v1:
time: 116 us; the launch traced here: 115 us
  Pallas kernels  109 us (94%)
  local copies, waits for them, and re-layouts  5.47 us (5%)
    pallas_call x1, Pallas kernels, on_device(): pl.pallas_call(functools.partial(barotropic_kernel, n, ng, cap), out_shap...  52.6 us
    pallas_call x1, Pallas kernels, on_device(): pl.pallas_call(functools.partial(columns_kernel, n, ng, cap), grid=(SLOTS...  35.5 us
    pallas_call x1, Pallas kernels, on_device(): pl.pallas_call(functools.partial(strips_kernel, n, ng, cap), out_shape=(j...  21.2 us
    unnamed x3, local copies, waits for them, and re-layouts  5.47 us

profile of v1, /device:TPU:1, one launch (start us, length us, event | category | flops | bytes accessed | tf_op | source)
XLA Modules:
  0.0 115.4 jit_solution(2596811978798457859)
XLA Ops:
  0.6 1.8 %copy.11.depth_ref = s32[300,180]{1,0:T(8,128)} copy(s32[300,180]{0,1:T(8,128)} %param.13) | data formatting | bytes 432000 | tf_op args[6]
  2.4 21.2 %strips.1 = (s32[16,64,128]{2,1,0:T(8,128)}, s32[24,128]{1,0:T(8,128)}) custom-call(s32[18]{0:T(128)} %ids_ref.3, s32[300,180]{1,0:T(8,128)} %copy.11.depth_ref), custom_call_target="tpu_custom_call" | custom-call | tf_op jit(solution)/shard_map/strips/pallas_call | solution.py:751
  23.6 35.5 %columns.1 = (f32[18,30,3000]{2,1,0:T(8,128)}, f32[18,30,3000]{2,1,0:T(8,128)}, f32[16,56,128]{2,1,0:T(8,128)}) custom-call(s32[18]{0:T(128)} %ids_ref.3, f32[29]{0:T(128)} %dfac_ref.1, f32[18,3000]{1,0:T(8,128)} %flux_ref.1, s32[18,3000]{1,0:T(8,128)} %depth_ref.3, s32[16,64,128]{2,1,0:T(8,128)} %get-tuple-element.11.strips_ref, f32[18,30,3000]{2,1,0:T(8,128)} %heat_ref.1, ...), custom_call_target="tpu_custom_call" | custom-call | tf_op jit(solution)/shard_map/columns/pallas_call | solution.py:766
  59.2 52.6 %barotropic.1 = (f32[300,180]{1,0:T(8,128)}, f32[300,180]{1,0:T(8,128)}) custom-call(s32[24,128]{1,0:T(8,128)} %get-tuple-element.14.tab_ref, s32[300,180]{1,0:T(8,128)} %copy.11.depth_ref, f32[16,56,128]{2,1,0:T(8,128)} %get-tuple-element.15.msg_ref), custom_call_target="tpu_custom_call" | custom-call | tf_op jit(solution)/shard_map/barotropic/pallas_call | solution.py:796
  111.8 1.8 %copy.13 = f32[300,180]{0,1:T(8,128)} copy(f32[300,180]{1,0:T(8,128)} %get-tuple-element.20) | data formatting | bytes 432000
  113.6 1.8 %copy.14 = f32[300,180]{0,1:T(8,128)} copy(f32[300,180]{1,0:T(8,128)} %get-tuple-element.21) | data formatting | bytes 432000

commit v2 on v1

--- a/solution.py
+++ b/solution.py
@@ -21,6 +21,7 @@
 THERMAL = 0.6
 DAMPING = 0.05
 
+BIG = 56 * 2**20
 TOP = 16
 PLANE = 328
 UROWS = TOP + SPAN_N * 8
@@ -63,53 +64,156 @@
     return jnp.where(lane < 128 - shift, xa, xb), jnp.where(lane < 128 - shift, xb, xa)
 
 
-def barrier(peers):
+def message_rows(cap):
+    return cap * TILES + (cap * 3 + 7) // 8 * 8
+
+
+def greet(peers):
     sem = pltpu.get_barrier_semaphore()
     for peer in peers:
         pl.semaphore_signal(sem, inc=1, device_id=peer, device_id_type=MESH)
-    pl.semaphore_wait(sem, len(peers))
-
-
-def strips_kernel(n, ng, cap, ids_ref, depth_ref, all_ref, tab_ref, pa, pb, msg, edge, got,
-                  s1, r1, s2, r2):
+    return lambda: pl.semaphore_wait(sem, len(peers))
+
+
+class Exchange:
+    def __init__(self, n, ng, g, y, row_out, row_in, col_out, col_in, row_s, row_r, col_s, col_r):
+        self.n, self.ng, self.g, self.y = n, ng, g, y
+        self.row_out, self.row_in, self.col_out, self.col_in = row_out, row_in, col_out, col_in
+        self.row_s, self.row_r, self.col_s, self.col_r = row_s, row_r, col_s, col_r
+
+    def start_rows(self, k, north, north_folded, south):
+        n, ng, g, y = self.n, self.ng, self.g, self.y
+        top = lax.div(y + 1, ng)
+        flipped = flip_cols(*north_folded)
+        for half in range(2):
+            self.row_out[k, 0, half] = jnp.where(y == ng - 1, flipped[half], north[half])
+            self.row_out[k, 1, half] = south[half]
+        up = pltpu.make_async_remote_copy(
+            self.row_out.at[k, 0], self.row_in.at[k, top], self.row_s.at[k, 0], self.row_r.at[k, top],
+            device_id=(g + top * (n - 1 - 2 * g), y + 1 - top), device_id_type=MESH,
+        )
+        down = pltpu.make_async_remote_copy(
+            self.row_out.at[k, 1], self.row_in.at[k, 1], self.row_s.at[k, 1], self.row_r.at[k, 1],
+            device_id=(g, lax.rem(y + ng - 1, ng)), device_id_type=MESH,
+        )
+        up.start()
+
+        @pl.when(y > 0)
+        def _():
+            down.start()
+
+        return up, down
+
+    def wait_rows(self, k, up, down):
+        g, y, ng = self.g, self.y, self.ng
+        up.wait_send()
+
+        @pl.when(y > 0)
+        def _():
+            down.wait_send()
+            south = pltpu.make_async_remote_copy(
+                self.row_out.at[k, 1], self.row_in.at[k, 0], self.row_s.at[k, 1], self.row_r.at[k, 0],
+                device_id=(g, lax.rem(y + ng - 1, ng)), device_id_type=MESH,
+            )
+            south.wait_recv()
+
+        down.wait_recv()
+
+        @pl.when(y == 0)
+        def _():
+            self.row_in[k, 0] = jnp.zeros((2, 8, 128), F32)
+
+        return [self.row_in[k, 0, half] for half in range(2)], [self.row_in[k, 1, half] for half in range(2)]
+
+    def start_cols(self, k):
+        n, g, y = self.n, self.g, self.y
+        copies = []
+        for slot, target in ((0, lax.rem(g + 1, n)), (1, lax.rem(g + n - 1, n))):
+            copy = pltpu.make_async_remote_copy(
+                self.col_out.at[k, slot], self.col_in.at[k, slot], self.col_s.at[k, slot], self.col_r.at[k, slot],
+                device_id=(target, y), device_id_type=MESH,
+            )
+            copy.start()
+            copies.append(copy)
+        return copies
+
+
+    def halo_rows(self, k, plane):
+        sub = iota((8, 128), 0)
+        north = [plane[half, 312:320, :] for half in range(2)]
+        south = [plane[half, 16:24, :] for half in range(2)]
+        turned = [
+            jnp.where(
+                sub < 2,
+                jnp.where(sub == 0, sroll(v, -3), sroll(v, -1)),
+                jnp.where(sub == 2, sroll(v, 1), sroll(v, 3)),
+            )
+            for v in north
+        ]
+        return self.start_rows(k, north, turned, south)
+
+    def halo_cols(self, k, plane, rows):
+        sub = iota((8, 128), 0)
+        lane = iota((8, 128), 1)
+        below, above = self.wait_rows(k, *rows)
+        for half in range(2):
+            plane[half, 8:16, :] = sroll(below[half], 4)
+            plane[half, 312:320, :] = jnp.where(sub < 4, plane[half, 312:320, :], sroll(above[half], 4))
+        for part in range(2):
+            to_east = jnp.zeros((8, 128), F32)
+            to_west = jnp.zeros((8, 128), F32)
+            for t in range(32 * part, min(39, 32 * part + 32)):
+                first = 4 * (t - 32 * part)
+                here = (lane >= first) & (lane < first + 4)
+                rows = slice(8 + 8 * t, 16 + 8 * t)
+                to_east = jnp.where(here, lroll(plane[1, rows, :], first - (EAST - 4)), to_east)
+                to_west = jnp.where(here, lroll(plane[0, rows, :], first), to_west)
+            self.col_out[k, 0, 8 * part : 8 * part + 8, :] = to_east
+            self.col_out[k, 1, 8 * part : 8 * part + 8, :] = to_west
+        return self.start_cols(k)
+
+    def halo_end(self, k, plane, copies):
+        lane = iota((8, 128), 1)
+        for copy in copies:
+            copy.wait()
+        for part in range(2):
+            west = self.col_in[k, 0, 8 * part : 8 * part + 8, :]
+            east = self.col_in[k, 1, 8 * part : 8 * part + 8, :]
+            for t in range(32 * part, min(39, 32 * part + 32)):
+                first = 4 * (t - 32 * part)
+                rows = slice(8 + 8 * t, 16 + 8 * t)
+                plane[1, rows, :] = jnp.where(
+                    lane >= 124,
+                    lroll(west, 124 - first),
+                    jnp.where((lane >= EAST) & (lane < EAST + 4), lroll(east, EAST - first), plane[1, rows, :]),
+                )
+
+    def halo(self, k, plane):
+        self.halo_end(k, plane, self.halo_cols(k, plane, self.halo_rows(k, plane)))
+
+
+STRIP_ROWS = 48
+NEAR = 40
+
+
+def strips_kernel(n, ng, cap, ids_ref, dfac_ref, depth_hbm, slot_hbm, flux_hbm,
+                  all_ref, tab_ref, dpl, coef, nflat, fflat,
+                  depth_ref, slot_ref, flux_ref, pa, pb, msg, edge, got,
+                  row_out, row_in, col_out, col_in,
+                  own, s1, r1, s2, r2, s3, r3, row_s, row_r, col_s, col_r):
     g = lax.axis_index("gx")
     y = lax.axis_index("gy")
+    loads = [
+        pltpu.make_async_copy(src, dst, own.at[k])
+        for k, (src, dst) in enumerate(((depth_hbm, depth_ref), (slot_hbm, slot_ref), (flux_hbm, flux_ref)))
+    ]
+    for load in loads:
+        load.start()
     up, down = lax.rem(y + 1, ng), lax.rem(y + ng - 1, ng)
-    barrier([(lax.rem(g + k, n), y) for k in range(1, n)] + [(g, up), (g, down)])
-    pa[0:ROWS, :] = depth_ref[:, 0:128]
-    pb[0:ROWS, 0:EAST] = depth_ref[:, 128:COLS]
+    band = [(lax.rem(g + k, n), y) for k in range(1, n)]
+    everyone = greet(band + [(g, up), (g, down)])
+    exchange = Exchange(n, ng, g, y, row_out, row_in, col_out, col_in, row_s, row_r, col_s, col_r)
     lane = iota((8, 128), 1)
-    strips = [[jnp.zeros((8, 128), I32) for _ in range(2)] for _ in range(KX)]
-    ns = []
-    for i in range(SPAN_N):
-        off = SPAN_E * i % 128
-        a = pa[pl.ds(i, 8, stride=SPAN_N), :]
-        b = pb[pl.ds(i, 8, stride=SPAN_N), :]
-        cells = [a, a, jnp.where(lane < 64, b, a)]
-        here = (lane == off) | (lane == (off + SPAN_E - 1) % 128)
-        for bx in range(KX):
-            strips[bx][i // 32] = jnp.where(here, lroll(cells[bx], off - SPAN_E * bx), strips[bx][i // 32])
-        if i == 0:
-            ns = [lroll(cells[bx], -SPAN_E * bx) for bx in range(KX)]
-        if i == SPAN_N - 1:
-            ns = [
-                jnp.where(lane < SPAN_E, ns[bx], lroll(cells[bx], SPAN_E - SPAN_E * bx))
-                for bx in range(KX)
-            ]
-    for bx in range(KX):
-        for part, value in enumerate((strips[bx][0], strips[bx][1], ns[bx])):
-            msg[pl.ds(bx * 3 + part, 8, stride=9), :] = value
-    edge[...] = jnp.zeros((8, 128), I32)
-    for bx in range(KX):
-        edge[bx : bx + 1, :] = ns[bx][0:1]
-        edge[3 + bx : 4 + bx, :] = ns[bx][KY - 1 : KY]
-    copies = []
-    for slot, target in ((0, up), (1, down)):
-        copy = pltpu.make_async_remote_copy(
-            edge, got.at[slot], s1.at[slot], r1.at[slot], device_id=(g, target), device_id_type=MESH
-        )
-        copy.start()
-        copies.append(copy)
     row = iota((1, 128), 1)
     code = jnp.full((1, 128), -1, I32)
     owners = []
@@ -124,25 +228,106 @@
         owners.append(owner)
         value = (owner * 32 + by * KX + lax.rem(bx, KX)) * 32 + rank
         code = jnp.where(row == s, jnp.where(owner >= 0, value, -1), code)
-    msg[54:55, :] = code
-    for bx, place in enumerate((55, 62, 63)):
-        msg[place : place + 1, :] = lroll(lreverse(ns[bx]), -8)[KY - 1 : KY]
-    for copy in copies:
-        copy.wait()
-    msg[56:59, :] = got[1][0:3]
-    msg[59:62, :] = got[0][3:6]
+    loads[0].wait()
+    pa[0:ROWS, :] = depth_ref[:, 0:128]
+    pb[0:ROWS, 0:EAST] = depth_ref[:, 128:COLS]
+    rims = [jnp.zeros((8, 128), I32) for _ in range(KX)]
+    ns = []
+    for i in range(SPAN_N):
+        off = SPAN_E * i % 128
+        a = pa[pl.ds(i, 8, stride=SPAN_N), :]
+        b = pb[pl.ds(i, 8, stride=SPAN_N), :]
+        cells = [a, a, jnp.where(lane < 64, b, a)]
+        push = 0 if i < 32 else 1
+        first, last = (off + push) % 128, (off + SPAN_E - 1 - push) % 128
+        for bx in range(KX):
+            turn = off - SPAN_E * bx
+            rims[bx] = jnp.where(lane == first, lroll(cells[bx], turn + push), rims[bx])
+            rims[bx] = jnp.where(lane == last, lroll(cells[bx], turn - push), rims[bx])
+        if i == 0:
+            ns = [lroll(cells[bx], -SPAN_E * bx) for bx in range(KX)]
+        if i == SPAN_N - 1:
+            ns = [
+                jnp.where(lane < SPAN_E, ns[bx], lroll(cells[bx], SPAN_E - SPAN_E * bx))
+                for bx in range(KX)
+            ]
+    for bx in range(KX):
+        for part, value in enumerate((rims[bx], ns[bx])):
+            msg[pl.ds(bx * 2 + part, 8, stride=6), :] = value
+    msg[36:37, :] = code
+    edge[...] = jnp.zeros((8, 128), I32)
+    for bx in range(KX):
+        edge[bx : bx + 1, :] = ns[bx][0:1]
+        edge[3 + bx : 4 + bx, :] = ns[bx][KY - 1 : KY]
+    zero8 = jnp.zeros((8, 128), F32)
+    for half in range(2):
+        dpl[half, 0:16, :] = jnp.zeros((16, 128), F32)
+        dpl[half, 312:PLANE, :] = jnp.zeros((PLANE - 312, 128), F32)
+    dpl[0, TOP : TOP + ROWS, :] = depth_ref[:, 0:128].astype(F32)
+    dpl[1, TOP : TOP + ROWS, :] = jnp.zeros((ROWS, 128), F32)
+    dpl[1, TOP : TOP + ROWS, 0:EAST] = depth_ref[:, 128:COLS].astype(F32)
+
+    everyone()
     copies = []
-    for k in range(1, n):
-        target = lax.rem(g + k, n)
+    for slot, target in ((0, up), (1, down)):
         copy = pltpu.make_async_remote_copy(
-            msg.at[pl.ds(0, 64)], all_ref.at[g], s2.at[k], r2.at[k], device_id=(target, y), device_id_type=MESH
+            edge, got.at[slot], s1.at[slot], r1.at[slot], device_id=(g, target), device_id_type=MESH
         )
         copy.start()
         copies.append(copy)
-    all_ref[pl.ds(g, 1)] = msg[0:64, :][None]
+    rows = exchange.halo_rows(0, dpl)
+    sends = []
+    for k, peer in enumerate(band):
+        copy = pltpu.make_async_remote_copy(
+            msg.at[pl.ds(0, NEAR)], all_ref.at[g, pl.ds(0, NEAR)], s2.at[k], r2.at[k],
+            device_id=peer, device_id_type=MESH,
+        )
+        copy.start()
+        sends.append(copy)
+    gain = jnp.zeros((1, 128), F32)
+    for k in range(LEVELS):
+        above = dfac_ref[k - 1] if k > 0 else jnp.float32(0)
+        below = dfac_ref[k] if k + 1 < LEVELS else jnp.float32(0)
+        base = (1.0 + above) - above * gain
+        full = 1.0 / (base + below)
+        gain = below * full
+        coef[0, k : k + 1, :] = full
+        coef[1, k : k + 1, :] = 1.0 / base
+        coef[2, k : k + 1, :] = jnp.broadcast_to(above, (1, 128))
+        coef[3, k : k + 1, :] = gain
     for copy in copies:
         copy.wait()
-    codes = all_ref[:, 54, :]
+    near = edge
+    for bx in range(KX):
+        mirrored = lroll(lreverse(ns[bx]), -8)[KY - 1 : KY]
+        near[bx : bx + 1, :] = jnp.where(y == ng - 1, mirrored, got[1, bx : bx + 1, :])
+        near[3 + bx : 4 + bx, :] = got[0, 3 + bx : 4 + bx, :]
+    for k, peer in enumerate(band):
+        copy = pltpu.make_async_remote_copy(
+            near, all_ref.at[g, pl.ds(NEAR, 8)], s3.at[k], r3.at[k], device_id=peer, device_id_type=MESH
+        )
+        copy.start()
+        sends.append(copy)
+    cols = exchange.halo_cols(0, dpl, rows)
+    all_ref[pl.ds(g, 1), 0:NEAR] = msg[0:NEAR, :][None]
+    all_ref[pl.ds(g, 1), NEAR:STRIP_ROWS] = near[...][None]
+    loads[1].wait()
+    loads[2].wait()
+    for t in range(TILES):
+        width = min(128, CELLS - 128 * t)
+        span = slice(t * 128, t * 128 + width)
+        for first in (0, 8, 16):
+            number = min(8, SLOTS - first)
+            place = pl.ds(first * TILES + t, number, stride=TILES)
+            for src, dst, kind in ((slot_ref, nflat, I32), (flux_ref, fflat, F32)):
+                value = src[first : first + number, span]
+                if width < 128:
+                    value = jnp.concatenate([value, jnp.zeros((number, 128 - width), kind)], axis=1)
+                dst[place, :] = value
+    exchange.halo_end(0, dpl, cols)
+    for copy in sends:
+        copy.wait()
+    codes = all_ref[:, 36, :]
     key = codes >> 5
     rank = codes & 31
     source = iota((n, 128), 0)
@@ -164,8 +349,12 @@
     return jnp.where(iota(x.shape, 1) >= step, a, sroll(a, 1))
 
 
-def columns_kernel(n, ng, cap, ids_ref, dfac_ref, flux_ref, depth_ref, strips_ref, heat_ref, salt_ref,
-                   heat_out, salt_out, msg_ref, nflat, fflat, coef, jcol, inh, ins, yh, ys, oh, os_, count):
+STEP = 33
+AHEAD = 5
+
+
+def columns_kernel(n, ng, cap, ids_ref, coef, fflat, nflat, strips_ref, heat_hbm, salt_hbm,
+                   heat_out, salt_out, msg_ref, heat_in, salt_in, jcol, inh, ins, yh, ys, oh, os_, count, sems):
     step = pl.program_id(0)
     shape = (TILES, 128)
     row24 = iota(shape, 0)
@@ -174,50 +363,46 @@
     lane = iota((1, 128), 1)
     last = CELLS - 128 * (TILES - 1)
 
+    ring = AHEAD + 1
+
+    def loads(slot):
+        place = lax.rem(slot, ring)
+        return [
+            pltpu.make_async_copy(src.at[slot], dst.at[place], sems.at[place, which])
+            for which, (src, dst) in enumerate(((heat_hbm, heat_in), (salt_hbm, salt_in)))
+        ]
+
     @pl.when(step == 0)
     def _():
-        for t in range(TILES):
-            width = 128 if t < TILES - 1 else last
-            cols = slice(t * 128, t * 128 + width)
-            for first in (0, 8, 16):
-                rows = min(8, SLOTS - first)
-                place = pl.ds(first * TILES + t, rows, stride=TILES)
-                d = depth_ref[first : first + rows, cols]
-                f = flux_ref[first : first + rows, cols]
-                if width < 128:
-                    d = jnp.concatenate([d, jnp.zeros((rows, 128 - width), I32)], axis=1)
-                    f = jnp.concatenate([f, jnp.zeros((rows, 128 - width), F32)], axis=1)
-                nflat[place, :] = d
-                fflat[place, :] = f
-        gain = jnp.zeros((1, 128), F32)
-        for k in range(LEVELS):
-            above = dfac_ref[k - 1] if k > 0 else jnp.float32(0)
-            below = dfac_ref[k] if k + 1 < LEVELS else jnp.float32(0)
-            base = (1.0 + above) - above * gain
-            full = 1.0 / (base + below)
-            gain = below * full
-            coef[0, k : k + 1, :] = full
-            coef[1, k : k + 1, :] = 1.0 / base
-            coef[2, k : k + 1, :] = jnp.broadcast_to(above, (1, 128))
-            coef[3, k : k + 1, :] = gain
-        owner = cell.astype(F32)
-        whole = jnp.floor((owner + 0.5) * (1.0 / SPAN_E))
+        for slot in range(AHEAD):
+            for load in loads(slot):
+                load.start()
+        flat = cell.astype(F32)
+        whole = jnp.floor((flat + 0.5) * (1.0 / SPAN_E))
         jcol[...] = cell - whole.astype(I32) * SPAN_E
         for d in range(n):
             count[d] = 0
 
+    @pl.when(step + AHEAD < SLOTS)
+    def _():
+        for load in loads(step + AHEAD):
+            load.start()
+
+    for load in loads(step):
+        load.wait()
+    here = lax.rem(step, ring)
     for t in range(TILES):
         width = 128 if t < TILES - 1 else last
         cols = slice(t * 128, t * 128 + width)
-        inh[t * 32 : t * 32 + LEVELS, 0:width] = heat_ref[0, :, cols]
-        ins[t * 32 : t * 32 + LEVELS, 0:width] = salt_ref[0, :, cols]
+        inh[t * STEP : t * STEP + LEVELS, 0:width] = heat_in[here, :, cols]
+        ins[t * STEP : t * STEP + LEVELS, 0:width] = salt_in[here, :, cols]
 
     mine = pl.ds(pl.multiple_of(step * TILES, 8), TILES)
     depth = nflat[mine, :]
     wet = depth > 0
     h = s = None
     for k in range(LEVELS):
-        level = pl.ds(k, TILES, stride=32)
+        level = pl.ds(k, TILES, stride=STEP)
         rh = inh[level, :]
         rs = ins[level, :]
         deeper = depth > k + 1
@@ -237,21 +422,21 @@
             yh[k * TILES : (k + 1) * TILES, :] = h
             ys[k * TILES : (k + 1) * TILES, :] = s
         wet = deeper
-    level = pl.ds(LEVELS - 1, TILES, stride=32)
+    level = pl.ds(LEVELS - 1, TILES, stride=STEP)
     oh[level, :] = h
     os_[level, :] = s
     for k in range(LEVELS - 2, -1, -1):
         gain = jnp.where(depth > k + 1, coef[3, k : k + 1, :], 0.0)
         h = yh[k * TILES : (k + 1) * TILES, :] + gain * h
         s = ys[k * TILES : (k + 1) * TILES, :] + gain * s
-        level = pl.ds(k, TILES, stride=32)
+        level = pl.ds(k, TILES, stride=STEP)
         oh[level, :] = h
         os_[level, :] = s
     for t in range(TILES):
         width = 128 if t < TILES - 1 else last
         cols = slice(t * 128, t * 128 + width)
-        heat_out[0, :, cols] = oh[t * 32 : t * 32 + LEVELS, 0:width]
-        salt_out[0, :, cols] = os_[t * 32 : t * 32 + LEVELS, 0:width]
+        heat_out[0, :, cols] = oh[t * STEP : t * STEP + LEVELS, 0:width]
+        salt_out[0, :, cols] = os_[t * STEP : t * STEP + LEVELS, 0:width]
 
     blocks_x = KX * n
     ident = ids_ref[step]
@@ -265,14 +450,14 @@
     def strip(device, place):
         return strips_ref[device, pl.ds(place, 1), :]
 
-    def sides(col, part):
-        return strip(lax.div(col, KX), (byl * KX + lax.rem(col, KX)) * 3 + part)
-
-    east = lax.rem(bx + 1, blocks_x)
-    west = lax.rem(bx + blocks_x - 1, blocks_x)
+    def rim_of(col):
+        return strip(lax.div(col, KX), (byl * KX + lax.rem(col, KX)) * 2)
+
+    east = rim_of(lax.rem(bx + 1, blocks_x))
+    west = rim_of(lax.rem(bx + blocks_x - 1, blocks_x))
     ew = [
-        jnp.where((lane & 3) == 3, lroll(sides(east, part), SPAN_E - 1), lroll(sides(west, part), 1 - SPAN_E))
-        for part in range(2)
+        jnp.where((lane & 3) == 3, lroll(east, SPAN_E - 1 - push), lroll(west, 1 - SPAN_E + push))
+        for push in range(2)
     ]
     ew = jnp.where(row24 < 15, ew[0], ew[1])
     mirror = blocks_x - 1 - bx
@@ -282,11 +467,11 @@
     north_dev = jnp.where(folded, lax.div(mirror, KX), dev)
     north_row = jnp.where(
         inner,
-        ((byl + 1) * KX + bxl) * 3 + 2,
-        jnp.where(folded, jnp.where(mirrored == 0, 55, 61 + mirrored), 56 + bxl),
+        ((byl + 1) * KX + bxl) * 2 + 1,
+        jnp.where(folded, NEAR + mirrored, NEAR + bxl),
     )
     north = lroll(strip(north_dev, north_row), -4)
-    south_row = jnp.where(byl > 0, ((byl - 1) * KX + bxl) * 3 + 2, 59 + bxl)
+    south_row = jnp.where(byl > 0, ((byl - 1) * KX + bxl) * 2 + 1, NEAR + 3 + bxl)
     south = jnp.where(by > 0, lroll(strip(dev, south_row), -SPAN_E), 0)
     j = jcol[...]
     inside = cell < CELLS
@@ -304,7 +489,7 @@
     pressure = jnp.zeros(shape, F32)
     total = jnp.zeros(shape, F32)
     for k in range(LEVELS):
-        level = pl.ds(k, TILES, stride=32)
+        level = pl.ds(k, TILES, stride=STEP)
         pressure = pressure + (HALINE * os_[level, :] - THERMAL * oh[level, :])
         total = total + pressure
         sums = [jnp.where(face == k + 1, total, held) for face, held in zip(faces, sums)]
@@ -332,126 +517,23 @@
             msg_ref[dev, pl.ds(base + part, 1), :] = value
 
 
-def barotropic_kernel(n, ng, cap, tab_ref, depth_ref, msg_ref, height_ref, misfit_ref,
-                      recv, blk, dpl, upl, zpl, wts, qpl, row_out, row_in, col_out, col_in,
+def barotropic_kernel(n, ng, cap, tab_ref, dpl, msg_ref, height_ref, misfit_ref,
+                      recv, blk, upl, zpl, wts, qpl, row_out, row_in, col_out, col_in,
                       red_out, red_x, red_y, own_sem, a2a_s, a2a_r, row_s, row_r, col_s, col_r,
                       rx_s, rx_r, ry_s, ry_r):
     g = lax.axis_index("gx")
     y = lax.axis_index("gy")
     band = [(lax.rem(g + k, n), y) for k in range(1, n)]
     column = [(g, lax.rem(y + k, ng)) for k in range(1, ng)]
-    barrier(band + column)
-    own = pltpu.make_async_copy(msg_ref.at[g], recv.at[g], own_sem)
-    own.start()
-    sends = []
-    for k, peer in enumerate(band):
-        copy = pltpu.make_async_remote_copy(
-            msg_ref.at[peer[0]], recv.at[g], a2a_s.at[k], a2a_r.at[k], device_id=peer, device_id_type=MESH
-        )
-        copy.start()
-        sends.append(copy)
-
+    everyone = greet(band + column)
+    exchange = Exchange(n, ng, g, y, row_out, row_in, col_out, col_in, row_s, row_r, col_s, col_r)
     lane = iota((8, 128), 1)
     sub = iota((8, 128), 0)
-    at_top = lax.div(y + 1, ng)
-    is_top = y == ng - 1
-    has_south = y > 0
-
-    def rows_start(k, north, north_folded, south):
-        flipped = flip_cols(*north_folded)
-        for half in range(2):
-            row_out[k, 0, half] = jnp.where(is_top, flipped[half], north[half])
-            row_out[k, 1, half] = south[half]
-        up = pltpu.make_async_remote_copy(
-            row_out.at[k, 0], row_in.at[k, at_top], row_s.at[k, 0], row_r.at[k, at_top],
-            device_id=(g + at_top * (n - 1 - 2 * g), y + 1 - at_top), device_id_type=MESH,
-        )
-        down = pltpu.make_async_remote_copy(
-            row_out.at[k, 1], row_in.at[k, 1], row_s.at[k, 1], row_r.at[k, 1],
-            device_id=(g, lax.rem(y + ng - 1, ng)), device_id_type=MESH,
-        )
-        up.start()
-
-        @pl.when(has_south)
-        def _():
-            down.start()
-
-        return up, down
-
-    def rows_wait(k, up, down):
-        up.wait_send()
-
-        @pl.when(has_south)
-        def _():
-            down.wait_send()
-            south = pltpu.make_async_remote_copy(
-                row_out.at[k, 1], row_in.at[k, 0], row_s.at[k, 1], row_r.at[k, 0],
-                device_id=(g, lax.rem(y + ng - 1, ng)), device_id_type=MESH,
-            )
-            south.wait_recv()
-
-        down.wait_recv()
-
-        @pl.when(jnp.logical_not(has_south))
-        def _():
-            row_in[k, 0] = jnp.zeros((2, 8, 128), F32)
-
-        return [row_in[k, 0, half] for half in range(2)], [row_in[k, 1, half] for half in range(2)]
-
-    def cols_start(k):
-        copies = []
-        for slot, target in ((0, lax.rem(g + 1, n)), (1, lax.rem(g + n - 1, n))):
-            copy = pltpu.make_async_remote_copy(
-                col_out.at[k, slot], col_in.at[k, slot], col_s.at[k, slot], col_r.at[k, slot],
-                device_id=(target, y), device_id_type=MESH,
-            )
-            copy.start()
-            copies.append(copy)
-        return copies
-
-    def halo(k, plane):
-        north = [plane[half, 312:320, :] for half in range(2)]
-        south = [plane[half, 16:24, :] for half in range(2)]
-        turned = [
-            jnp.where(sub == 0, sroll(v, -3), jnp.where(sub == 1, sroll(v, -1), sroll(v, 1))) for v in north
-        ]
-        below, above = rows_wait(k, *rows_start(k, north, turned, south))
-        for half in range(2):
-            plane[half, 8:16, :] = sroll(below[half], 4)
-            plane[half, 312:320, :] = jnp.where(sub < 4, north[half], sroll(above[half], 4))
-        to_east = jnp.zeros((8, 128), F32)
-        to_west = jnp.zeros((8, 128), F32)
-        for t in range(39):
-            here = (lane >= 3 * t) & (lane < 3 * t + 3)
-            rows = slice(8 + 8 * t, 16 + 8 * t)
-            to_east = jnp.where(here, lroll(plane[1, rows, :], 3 * t - (EAST - 3)), to_east)
-            to_west = jnp.where(here, lroll(plane[0, rows, :], 3 * t), to_west)
-        col_out[k, 0, 0:8, :] = to_east
-        col_out[k, 1, 0:8, :] = to_west
-        for copy in cols_start(k):
-            copy.wait()
-        from_west = col_in[k, 0, 0:8, :]
-        from_east = col_in[k, 1, 0:8, :]
-        for t in range(39):
-            rows = slice(8 + 8 * t, 16 + 8 * t)
-            plane[1, rows, :] = jnp.where(
-                lane >= 125,
-                lroll(from_west, 125 - 3 * t),
-                jnp.where((lane >= EAST) & (lane < EAST + 3), lroll(from_east, EAST - 3 * t), plane[1, rows, :]),
-            )
-
     zero8 = jnp.zeros((8, 128), F32)
-    for half in range(2):
-        dpl[half, 0:16, :] = jnp.zeros((16, 128), F32)
-        dpl[half, 312:PLANE, :] = jnp.zeros((PLANE - 312, 128), F32)
-    dpl[0, TOP : TOP + ROWS, :] = depth_ref[:, 0:128].astype(F32)
-    dpl[1, TOP : TOP + ROWS, :] = jnp.zeros((ROWS, 128), F32)
-    dpl[1, TOP : TOP + ROWS, 0:EAST] = depth_ref[:, 128:COLS].astype(F32)
     for half in range(2):
         for ref in (zpl, qpl.at[0], qpl.at[1], qpl.at[2], qpl.at[3]):
             ref[half, 0:8, :] = zero8
             ref[half, 320:PLANE, :] = zero8
-    halo(0, dpl)
 
     span = 24
     chunks = 13
@@ -494,6 +576,18 @@
 
     lax.fori_loop(0, chunks, weigh, 0)
 
+    everyone()
+    own = pltpu.make_async_copy(msg_ref.at[g], recv.at[g], own_sem)
+    own.start()
+    sends = []
+    for k, peer in enumerate(band):
+        copy = pltpu.make_async_remote_copy(
+            msg_ref.at[peer[0]], recv.at[g], a2a_s.at[k], a2a_r.at[k], device_id=peer, device_id_type=MESH
+        )
+        copy.start()
+        sends.append(copy)
+
+
     own.wait()
     for copy in sends:
         copy.wait()
@@ -529,8 +623,8 @@
 
     rims = [[rows_of(bx, TILES + part) for part in range(2)] for bx in range(KX)]
     for part in range(2):
-        col_out[1, 0, 8 * part : 8 * part + 8, :] = rims[KX - 1][part]
-        col_out[1, 1, 8 * part : 8 * part + 8, :] = rims[0][part]
+        col_out[0, 0, 8 * part : 8 * part + 8, :] = rims[KX - 1][part]
+        col_out[0, 1, 8 * part : 8 * part + 8, :] = rims[0][part]
     cap_rows = [rows_of(bx, TILES + 2) for bx in range(KX)]
 
     def lay(v):
@@ -539,8 +633,8 @@
 
     souths = lay([lroll(cap_rows[bx], SPAN_E * bx) for bx in range(KX)])
     norths = lay([lroll(cap_rows[bx], SPAN_E * bx - SPAN_E) for bx in range(KX)])
-    waits = rows_start(1, norths, [sroll(v, 8 - (KY - 1)) for v in norths], souths)
-    col_copies = cols_start(1)
+    waits = exchange.start_rows(0, norths, [sroll(v, 8 - (KY - 1)) for v in norths], souths)
+    col_copies = exchange.start_cols(0)
     for i in range(SPAN_N):
         t, off = SPAN_E * i // 128, SPAN_E * i % 128
         cells = []
@@ -568,7 +662,7 @@
             second = second + jnp.where((sub > 0) & (sub < KY), sroll(norths[1], 1), 0.0)
         upl[0, pl.ds(TOP + i, 8, stride=SPAN_N), :] = first
         upl[1, pl.ds(TOP + i, 8, stride=SPAN_N), :] = second
-    below, above = rows_wait(1, *waits)
+    below, above = exchange.wait_rows(0, *waits)
     for copy in col_copies:
         copy.wait()
     for half in range(2):
@@ -580,8 +674,8 @@
         off = SPAN_E * i % 128
         part = slice(8 * (i // 32), 8 * (i // 32) + 8)
         rows = pl.ds(TOP + i, 8, stride=SPAN_N)
-        west = lroll(col_in[1, 0, part, :], 1 - SPAN_E - off)
-        east = lroll(col_in[1, 1, part, :], COLS - 1 - off)
+        west = lroll(col_in[0, 0, part, :], 1 - SPAN_E - off)
+        east = lroll(col_in[0, 1, part, :], COLS - 1 - off)
         good = sub < KY
         upl[0, rows, :] = upl[0, rows, :] + jnp.where((lane == 0) & good, west, 0.0)
         upl[1, rows, :] = upl[1, rows, :] + jnp.where((lane == EAST - 1) & good, east, 0.0)
@@ -595,7 +689,7 @@
         return carry
 
     lax.fori_loop(0, chunks, begin, 0)
-    halo(2, zpl)
+    exchange.halo(1, zpl)
 
     def image(out, scale_next):
         def body(t, carry):
@@ -741,29 +835,45 @@
     finish(ROWS // span * span, ROWS % span)
 
 
-def on_device(n, ng, heat, salt, flux, dfac, ids, slot_depth, grid_depth):
-    cap = (SLOTS + n - 1) // n
-    msg_rows = cap * TILES + (cap * 3 + 7) // 8 * 8
+def strips_call(n, ng, flux, dfac, ids, slot_depth, grid_depth):
     vmem = pl.BlockSpec(memory_space=VMEM)
     smem = pl.BlockSpec(memory_space=pltpu.SMEM)
+    hbm = pl.BlockSpec(memory_space=pl.ANY)
     dma = pltpu.SemaphoreType.DMA
-    big = 56 * 2**20
-    strips, table = pl.pallas_call(
-        functools.partial(strips_kernel, n, ng, cap),
-        out_shape=(jax.ShapeDtypeStruct((n, 64, 128), I32), jax.ShapeDtypeStruct((24, 128), I32)),
-        in_specs=[smem, vmem],
-        out_specs=(vmem, vmem),
+    flat = (SLOTS * TILES, 128)
+    return pl.pallas_call(
+        functools.partial(strips_kernel, n, ng, (SLOTS + n - 1) // n),
+        out_shape=(
+            jax.ShapeDtypeStruct((n, STRIP_ROWS, 128), I32), jax.ShapeDtypeStruct((24, 128), I32),
+            jax.ShapeDtypeStruct((2, PLANE, 128), F32), jax.ShapeDtypeStruct((4, 32, 128), F32),
+            jax.ShapeDtypeStruct(flat, I32), jax.ShapeDtypeStruct(flat, F32),
+        ),
+        in_specs=[smem, smem, hbm, hbm, hbm],
+        out_specs=(vmem,) * 6,
         scratch_shapes=[
-            VMEM((400, 128), I32), VMEM((400, 128), I32), VMEM((72, 128), I32), VMEM((8, 128), I32),
-            VMEM((2, 8, 128), I32), dma((2,)), dma((2,)), dma((n,)), dma((n,)),
+            VMEM((ROWS, COLS), I32), VMEM((SLOTS, CELLS), I32), VMEM((SLOTS, CELLS), F32),
+            VMEM((400, 128), I32), VMEM((400, 128), I32), VMEM((48, 128), I32), VMEM((8, 128), I32),
+            VMEM((2, 8, 128), I32),
+            VMEM((1, 2, 2, 8, 128), F32), VMEM((1, 2, 2, 8, 128), F32),
+            VMEM((1, 2, 16, 128), F32), VMEM((1, 2, 16, 128), F32),
+            dma((3,)), dma((2,)), dma((2,)), dma((n,)), dma((n,)), dma((n,)), dma((n,)),
+            dma((1, 2)), dma((1, 2)), dma((1, 2)), dma((1, 2)),
         ],
-        compiler_params=pltpu.CompilerParams(collective_id=0, has_side_effects=True, vmem_limit_bytes=big),
+        compiler_params=pltpu.CompilerParams(collective_id=0, has_side_effects=True, vmem_limit_bytes=BIG),
         name="strips",
-    )(ids, grid_depth)
-
-    whole = lambda s: (0, 0)
+    )(ids, dfac, grid_depth, slot_depth, flux)
+
+
+def columns_call(n, ng, heat, salt, ids, coef, fflat, nflat, strips):
+    cap = (SLOTS + n - 1) // n
+    msg_rows = message_rows(cap)
+    smem = pl.BlockSpec(memory_space=pltpu.SMEM)
+    hbm = pl.BlockSpec(memory_space=pl.ANY)
+    fixed = lambda shape: pl.BlockSpec(shape, lambda s: (0,) * len(shape))
     block = pl.BlockSpec((1, LEVELS, CELLS), lambda s: (s, 0, 0))
-    heat_new, salt_new, msg = pl.pallas_call(
+    ring = (AHEAD + 1, LEVELS, CELLS)
+    tall = TILES * STEP + 8
+    return pl.pallas_call(
         functools.partial(columns_kernel, n, ng, cap),
         grid=(SLOTS,),
         out_shape=(
@@ -772,45 +882,52 @@
             jax.ShapeDtypeStruct((n, msg_rows, 128), F32),
         ),
         in_specs=[
-            smem, smem,
-            pl.BlockSpec((SLOTS, CELLS), whole),
-            pl.BlockSpec((SLOTS, CELLS), whole),
-            pl.BlockSpec((n, 64, 128), lambda s: (0, 0, 0)),
-            block, block,
+            smem, fixed((4, 32, 128)), fixed((SLOTS * TILES, 128)), fixed((SLOTS * TILES, 128)),
+            fixed((n, STRIP_ROWS, 128)), hbm, hbm,
         ],
-        out_specs=(block, block, pl.BlockSpec((n, msg_rows, 128), lambda s: (0, 0, 0))),
+        out_specs=(block, block, fixed((n, msg_rows, 128))),
         scratch_shapes=[
-            VMEM((SLOTS * TILES, 128), I32), VMEM((SLOTS * TILES, 128), F32), VMEM((4, 32, 128), F32),
-            VMEM((TILES, 128), I32),
-            VMEM((TILES * 32, 128), F32), VMEM((TILES * 32, 128), F32),
+            VMEM(ring, F32), VMEM(ring, F32), VMEM((TILES, 128), I32),
+            VMEM((tall, 128), F32), VMEM((tall, 128), F32),
             VMEM((TILES * LEVELS, 128), F32), VMEM((TILES * LEVELS, 128), F32),
-            VMEM((TILES * 32, 128), F32), VMEM((TILES * 32, 128), F32),
-            pltpu.SMEM((n,), I32),
+            VMEM((tall, 128), F32), VMEM((tall, 128), F32),
+            pltpu.SMEM((n,), I32), pltpu.SemaphoreType.DMA((AHEAD + 1, 2)),
         ],
-        compiler_params=pltpu.CompilerParams(vmem_limit_bytes=big),
+        compiler_params=pltpu.CompilerParams(vmem_limit_bytes=BIG),
         name="columns",
-    )(ids, dfac, flux, slot_depth, strips, heat, salt)
-
+    )(ids, coef, fflat, nflat, strips, heat, salt)
+
+
+def barotropic_call(n, ng, table, depths, msg):
+    cap = (SLOTS + n - 1) // n
+    vmem = pl.BlockSpec(memory_space=VMEM)
+    dma = pltpu.SemaphoreType.DMA
     field = jax.ShapeDtypeStruct((ROWS, COLS), F32)
     plane = (2, PLANE, 128)
-    height, misfit = pl.pallas_call(
+    return pl.pallas_call(
         functools.partial(barotropic_kernel, n, ng, cap),
         out_shape=(field, field),
         in_specs=[vmem, vmem, pl.BlockSpec(memory_space=pl.ANY)],
         out_specs=(vmem, vmem),
         scratch_shapes=[
-            VMEM((n, msg_rows, 128), F32), VMEM((KX * 8 * BLK, 128), F32),
-            VMEM(plane, F32), VMEM((2, UROWS, 128), F32), VMEM(plane, F32),
+            VMEM((n, message_rows(cap), 128), F32), VMEM((KX * 8 * BLK, 128), F32),
+            VMEM((2, UROWS, 128), F32), VMEM(plane, F32),
             VMEM((7,) + plane, F32), VMEM((4,) + plane, F32),
-            VMEM((3, 2, 2, 8, 128), F32), VMEM((3, 2, 2, 8, 128), F32),
-            VMEM((3, 2, 16, 128), F32), VMEM((3, 2, 16, 128), F32),
+            VMEM((2, 2, 2, 8, 128), F32), VMEM((2, 2, 2, 8, 128), F32),
+            VMEM((2, 2, 16, 128), F32), VMEM((2, 2, 16, 128), F32),
             VMEM((2, 2, 8, 128), F32), VMEM((2, n, 8, 128), F32), VMEM((2, ng, 8, 128), F32),
-            dma, dma((n,)), dma((n,)), dma((3, 2)), dma((3, 2)), dma((3, 2)), dma((3, 2)),
+            dma, dma((n,)), dma((n,)), dma((2, 2)), dma((2, 2)), dma((2, 2)), dma((2, 2)),
             dma((2, n)), dma((2, n)), dma((2, ng)), dma((2, ng)),
         ],
-        compiler_params=pltpu.CompilerParams(collective_id=1, has_side_effects=True, vmem_limit_bytes=big),
+        compiler_params=pltpu.CompilerParams(collective_id=1, has_side_effects=True, vmem_limit_bytes=BIG),
         name="barotropic",
-    )(table, grid_depth, msg)
+    )(table, depths, msg)
+
+
+def on_device(n, ng, heat, salt, flux, dfac, ids, slot_depth, grid_depth):
+    strips, table, depths, coef, nflat, fflat = strips_call(n, ng, flux, dfac, ids, slot_depth, grid_depth)
+    heat_new, salt_new, msg = columns_call(n, ng, heat, salt, ids, coef, fflat, nflat, strips)
+    height, misfit = barotropic_call(n, ng, table, depths, msg)
     return heat_new, salt_new, height, misfit
 
 

time: 116 us -> 88.9 us (0.77)
  Pallas kernels: 109 us -> 82.4 us
    pallas_call x3, Pallas kernels: 109 us -> 82.4 us  [the longest x1 49.1 us: barotropic_call(): pl.pallas_call(functools.partial(barotropic_kernel, n, ng, cap), out_shap...]
where the time goes in v2:
time: 88.9 us; the launch traced here: 88.5 us
  Pallas kernels  82.4 us (93%)
  local copies, waits for them, and re-layouts  5.47 us (6%)
    pallas_call x1, Pallas kernels, barotropic_call(): pl.pallas_call(functools.partial(barotropic_kernel, n, ng, cap), out_shap...  49.1 us
    pallas_call x1, Pallas kernels, strips_call(): pl.pallas_call(functools.partial(strips_kernel, n, ng, (SLOTS + n - 1) //...  16.9 us
    pallas_call x1, Pallas kernels, columns_call(): pl.pallas_call(functools.partial(columns_kernel, n, ng, cap), grid=(SLOTS...  16.4 us
    unnamed x3, local copies, waits for them, and re-layouts  5.47 us

profile of v2, /device:TPU:1, one launch (start us, length us, event | category | flops | bytes accessed | tf_op | source)
XLA Modules:
  0.0 88.5 jit_solution(2495894610824168615)
XLA Ops:
  0.6 1.8 %copy.11.depth_hbm = s32[300,180]{1,0:T(8,128)} copy(s32[300,180]{0,1:T(8,128)} %param.13) | data formatting | bytes 432000 | tf_op args[6]
  2.5 16.9 %strips.1 = (s32[16,48,128]{2,1,0:T(8,128)}, s32[24,128]{1,0:T(8,128)}, f32[2,328,128]{2,1,0:T(8,128)}, f32[4,32,128]{2,1,0:T(8,128)}, s32[432,128]{1,0:T(8,128)}, /*index=5*/f32[432,128]{1,0:T(8,128)}) custom-call(s32[18]{0:T(128)} %ids_ref.3, f32[29]{0:T(128)} %dfac_ref.1, s32[300,180]{1,0:T(8,128)} %copy.11.depth_hbm, s32[18,3000]{1,0:T(8,128)} %slot_hbm.1, ...), custom_call_target="tpu_custom_call" | custom-call | tf_op jit(solution)/shard_map/strips/pallas_call | solution.py:844
  19.3 16.4 %columns.1 = (f32[18,30,3000]{2,1,0:T(8,128)}, f32[18,30,3000]{2,1,0:T(8,128)}, f32[16,56,128]{2,1,0:T(8,128)}) custom-call(s32[18]{0:T(128)} %ids_ref.3, f32[4,32,128]{2,1,0:T(8,128)} %get-tuple-element.15.coef, f32[432,128]{1,0:T(8,128)} %get-tuple-element.16.fflat, s32[432,128]{1,0:T(8,128)} %get-tuple-element.17.nflat, ...), custom_call_target="tpu_custom_call" | custom-call | tf_op jit(solution)/shard_map/columns/pallas_call | solution.py:876
  35.7 49.1 %barotropic.1 = (f32[300,180]{1,0:T(8,128)}, f32[300,180]{1,0:T(8,128)}) custom-call(s32[24,128]{1,0:T(8,128)} %get-tuple-element.21.tab_ref, f32[2,328,128]{2,1,0:T(8,128)} %get-tuple-element.22.dpl, f32[16,56,128]{2,1,0:T(8,128)} %get-tuple-element.23.msg_ref), custom_call_target="tpu_custom_call" | custom-call | tf_op jit(solution)/shard_map/barotropic/pallas_call | solution.py:907
  84.9 1.8 %copy.12 = f32[300,180]{0,1:T(8,128)} copy(f32[300,180]{1,0:T(8,128)} %get-tuple-element.28) | data formatting | bytes 432000
  86.7 1.8 %copy.13 = f32[300,180]{0,1:T(8,128)} copy(f32[300,180]{1,0:T(8,128)} %get-tuple-element.29) | data formatting | bytes 432000

commit v3 on v2

--- a/solution.py
+++ b/solution.py
@@ -80,66 +80,40 @@
         self.n, self.ng, self.g, self.y = n, ng, g, y
         self.row_out, self.row_in, self.col_out, self.col_in = row_out, row_in, col_out, col_in
         self.row_s, self.row_r, self.col_s, self.col_r = row_s, row_r, col_s, col_r
-
-    def start_rows(self, k, north, north_folded, south):
-        n, ng, g, y = self.n, self.ng, self.g, self.y
-        top = lax.div(y + 1, ng)
-        flipped = flip_cols(*north_folded)
-        for half in range(2):
-            self.row_out[k, 0, half] = jnp.where(y == ng - 1, flipped[half], north[half])
-            self.row_out[k, 1, half] = south[half]
-        up = pltpu.make_async_remote_copy(
-            self.row_out.at[k, 0], self.row_in.at[k, top], self.row_s.at[k, 0], self.row_r.at[k, top],
-            device_id=(g + top * (n - 1 - 2 * g), y + 1 - top), device_id_type=MESH,
-        )
-        down = pltpu.make_async_remote_copy(
-            self.row_out.at[k, 1], self.row_in.at[k, 1], self.row_s.at[k, 1], self.row_r.at[k, 1],
-            device_id=(g, lax.rem(y + ng - 1, ng)), device_id_type=MESH,
-        )
-        up.start()
-
-        @pl.when(y > 0)
-        def _():
-            down.start()
-
-        return up, down
-
-    def wait_rows(self, k, up, down):
-        g, y, ng = self.g, self.y, self.ng
-        up.wait_send()
-
-        @pl.when(y > 0)
-        def _():
-            down.wait_send()
-            south = pltpu.make_async_remote_copy(
-                self.row_out.at[k, 1], self.row_in.at[k, 0], self.row_s.at[k, 1], self.row_r.at[k, 0],
-                device_id=(g, lax.rem(y + ng - 1, ng)), device_id_type=MESH,
+        self.lane, self.sub = iota((8, 128), 1), iota((8, 128), 0)
+        self.top = lax.div(y + 1, ng)
+
+    def copies(self, k):
+        n, ng, g, y, top = self.n, self.ng, self.g, self.y, self.top
+        center = g + top * (n - 1 - 2 * g)
+        result = []
+        for place, d in ((0, 0), (1, 1), (2, -1)):
+            target = lax.rem(center + d + n, n)
+            up = pltpu.make_async_remote_copy(
+                self.row_out.at[k, 0], self.row_in.at[k, top, place], self.row_s.at[k, 0, place],
+                self.row_r.at[k, top, place], device_id=(target, y + 1 - top), device_id_type=MESH,
             )
-            south.wait_recv()
-
-        down.wait_recv()
-
-        @pl.when(y == 0)
-        def _():
-            self.row_in[k, 0] = jnp.zeros((2, 8, 128), F32)
-
-        return [self.row_in[k, 0, half] for half in range(2)], [self.row_in[k, 1, half] for half in range(2)]
-
-    def start_cols(self, k):
-        n, g, y = self.n, self.g, self.y
-        copies = []
-        for slot, target in ((0, lax.rem(g + 1, n)), (1, lax.rem(g + n - 1, n))):
-            copy = pltpu.make_async_remote_copy(
+            down, under = [
+                pltpu.make_async_remote_copy(
+                    self.row_out.at[k, 1], self.row_in.at[k, into, place], self.row_s.at[k, 1, place],
+                    self.row_r.at[k, into, place],
+                    device_id=(lax.rem(g + d + n, n), lax.rem(y + ng - 1, ng)), device_id_type=MESH,
+                )
+                for into in (1, 0)
+            ]
+            mine = None if d == 0 else (y == ng - 1) & (target == g)
+            result.append((place, up, down, under, mine))
+        cols = [
+            pltpu.make_async_remote_copy(
                 self.col_out.at[k, slot], self.col_in.at[k, slot], self.col_s.at[k, slot], self.col_r.at[k, slot],
                 device_id=(target, y), device_id_type=MESH,
             )
-            copy.start()
-            copies.append(copy)
-        return copies
-
-
-    def halo_rows(self, k, plane):
-        sub = iota((8, 128), 0)
+            for slot, target in ((0, lax.rem(g + 1, n)), (1, lax.rem(g + n - 1, n)))
+        ]
+        return result, cols
+
+    def pack(self, k, plane, caps=None):
+        lane, sub = self.lane, self.sub
         north = [plane[half, 312:320, :] for half in range(2)]
         south = [plane[half, 16:24, :] for half in range(2)]
         turned = [
@@ -150,15 +124,18 @@
             )
             for v in north
         ]
-        return self.start_rows(k, north, turned, south)
-
-    def halo_cols(self, k, plane, rows):
-        sub = iota((8, 128), 0)
-        lane = iota((8, 128), 1)
-        below, above = self.wait_rows(k, *rows)
+        if caps is not None:
+            for half in range(2):
+                north[half] = jnp.where(sub == 5, caps[0][half], north[half])
+                turned[half] = jnp.where(sub == 5, caps[0][half], turned[half])
+                south[half] = jnp.where(sub == 5, caps[1][half], south[half])
+        flipped = list(flip_cols(*turned))
+        flipped[1] = jnp.where(
+            lane == 60, lroll(turned[1], -1), jnp.where(lane == 61, lroll(turned[1], 1), flipped[1])
+        )
         for half in range(2):
-            plane[half, 8:16, :] = sroll(below[half], 4)
-            plane[half, 312:320, :] = jnp.where(sub < 4, plane[half, 312:320, :], sroll(above[half], 4))
+            self.row_out[k, 0, half] = jnp.where(self.y == self.ng - 1, flipped[half], north[half])
+            self.row_out[k, 1, half] = south[half]
         for part in range(2):
             to_east = jnp.zeros((8, 128), F32)
             to_west = jnp.zeros((8, 128), F32)
@@ -166,39 +143,126 @@
                 first = 4 * (t - 32 * part)
                 here = (lane >= first) & (lane < first + 4)
                 rows = slice(8 + 8 * t, 16 + 8 * t)
-                to_east = jnp.where(here, lroll(plane[1, rows, :], first - (EAST - 4)), to_east)
-                to_west = jnp.where(here, lroll(plane[0, rows, :], first), to_west)
+                a, b = plane[0, rows, :], plane[1, rows, :]
+                east, west = lroll(b, first - (EAST - 4)), lroll(a, first)
+                if caps is not None:
+                    east = jnp.where(lane == first + 3, lroll(b, first + 3 - 60), lroll(b, first - (EAST - 3)))
+                    west = jnp.where(lane == first + 3, lroll(b, first + 3 - 61), west)
+                to_east = jnp.where(here, east, to_east)
+                to_west = jnp.where(here, west, to_west)
+            if part == 1 and caps is not None:
+                here = (lane >= 64) & (lane < 67)
+                both = [jnp.where(sub == 0, caps[0][half], caps[1][half]) for half in range(2)]
+                to_east = jnp.where(here, lroll(both[1], 64 - (EAST - 3)), to_east)
+                to_west = jnp.where(here, lroll(both[0], 64), to_west)
             self.col_out[k, 0, 8 * part : 8 * part + 8, :] = to_east
             self.col_out[k, 1, 8 * part : 8 * part + 8, :] = to_west
-        return self.start_cols(k)
-
-    def halo_end(self, k, plane, copies):
-        lane = iota((8, 128), 1)
-        for copy in copies:
+
+    def start(self, k):
+        rows, cols = self.copies(k)
+        for copy in cols:
+            copy.start()
+        for place, up, down, under, mine in rows:
+            if mine is None:
+                up.start()
+            else:
+
+                @pl.when(jnp.logical_not(mine))
+                def _(up=up):
+                    up.start()
+
+                @pl.when(mine)
+                def _(place=place):
+                    self.row_in[k, 1, place] = self.row_out[k, 0]
+
+            @pl.when(self.y > 0)
+            def _(down=down):
+                down.start()
+
+        return rows, cols
+
+    def wait(self, k, started):
+        rows, cols = started
+        for copy in cols:
             copy.wait()
+        for place, up, down, under, mine in rows:
+            if mine is None:
+                up.wait_send()
+                down.wait_recv()
+            else:
+
+                @pl.when(jnp.logical_not(mine))
+                def _(up=up, down=down):
+                    up.wait_send()
+                    down.wait_recv()
+
+            @pl.when(self.y > 0)
+            def _(down=down, under=under):
+                down.wait_send()
+                under.wait_recv()
+
+            @pl.when(self.y == 0)
+            def _(place=place):
+                self.row_in[k, 0, place] = jnp.zeros((2, 8, 128), F32)
+
+    def unpack(self, k, plane, caps=None):
+        lane, sub = self.lane, self.sub
         for part in range(2):
             west = self.col_in[k, 0, 8 * part : 8 * part + 8, :]
             east = self.col_in[k, 1, 8 * part : 8 * part + 8, :]
-            for t in range(32 * part, min(39, 32 * part + 32)):
+            for t in range(max(1, 32 * part), min(39, 32 * part + 32)):
                 first = 4 * (t - 32 * part)
                 rows = slice(8 + 8 * t, 16 + 8 * t)
-                plane[1, rows, :] = jnp.where(
-                    lane >= 124,
-                    lroll(west, 124 - first),
-                    jnp.where((lane >= EAST) & (lane < EAST + 4), lroll(east, EAST - first), plane[1, rows, :]),
-                )
-
-    def halo(self, k, plane):
-        self.halo_end(k, plane, self.halo_cols(k, plane, self.halo_rows(k, plane)))
-
-
-STRIP_ROWS = 48
-NEAR = 40
+                value = plane[1, rows, :]
+                if caps is None:
+                    value = jnp.where(lane >= 124, lroll(west, 124 - first), value)
+                    value = jnp.where((lane >= EAST) & (lane < EAST + 4), lroll(east, EAST - first), value)
+                else:
+                    value = jnp.where(lane >= 125, lroll(west, 125 - first), value)
+                    value = jnp.where((lane >= EAST) & (lane < EAST + 3), lroll(east, EAST - first), value)
+                    value = jnp.where(lane == 62, lroll(east, 62 - first - 3), value)
+                    value = jnp.where(lane == 63, lroll(west, 63 - first - 3), value)
+                plane[1, rows, :] = value
+        found = []
+        for side in range(2):
+            c, w, e = [[self.row_in[k, side, place, half] for half in range(2)] for place in range(3)]
+            tail = jnp.where(lane >= 124, lroll(w[1], 76), c[1])
+            tail = jnp.where((lane >= EAST) & (lane < EAST + 4), lroll(e[0], EAST), tail)
+            tail = jnp.where(lane == 62, lroll(e[1], 1), jnp.where(lane == 63, lroll(w[1], 3), tail))
+            found.append((c[0], tail))
+        for half in range(2):
+            plane[half, 8:16, :] = sroll(found[0][half], 4)
+            plane[half, 312:320, :] = jnp.where(sub < 4, plane[half, 312:320, :], sroll(found[1][half], 4))
+        if caps is None:
+            return
+        west, east = self.col_in[k, 0, 8:16, :], self.col_in[k, 1, 8:16, :]
+        line = lane[0:1]
+        for half in range(2):
+            for which, row in ((0, 316), (1, 15)):
+                value = caps[which][half]
+                if half == 1:
+                    value = jnp.where(line >= 125, lroll(west, 125 - 64)[which : which + 1], value)
+                    value = jnp.where(
+                        (line >= EAST) & (line < EAST + 3), lroll(east, EAST - 64)[which : which + 1], value
+                    )
+                plane[half, row : row + 1, :] = plane[half, row : row + 1, :] + value
+            for side, row in ((1, 315), (0, 16)):
+                value = found[side][half][5:6]
+                if half == 1:
+                    value = jnp.where((line < EAST + 3) | (line >= 125), value, 0.0)
+                plane[half, row : row + 1, :] = plane[half, row : row + 1, :] + value
+
+
+IDS = 36
+MIRROR = 37
+SIBLING = 40
+OTHER = 48
+STRIP_ROWS = 56
 
 
 def strips_kernel(n, ng, cap, ids_ref, dfac_ref, depth_hbm, slot_hbm, flux_hbm,
                   all_ref, tab_ref, dpl, coef, nflat, fflat,
-                  depth_ref, slot_ref, flux_ref, pa, pb, msg, edge, got,
+                  depth_ref, slot_ref, flux_ref, wide, msg, edge, got,
                   row_out, row_in, col_out, col_in,
                   own, s1, r1, s2, r2, s3, r3, row_s, row_r, col_s, col_r):
     g = lax.axis_index("gx")
@@ -209,9 +273,13 @@
     ]
     for load in loads:
         load.start()
-    up, down = lax.rem(y + 1, ng), lax.rem(y + ng - 1, ng)
+    odd = lax.rem(y, 2)
+    sibling = y + 1 - 2 * odd
+    other = lax.rem(y + ng + 2 * odd - 1, ng)
     band = [(lax.rem(g + k, n), y) for k in range(1, n)]
-    everyone = greet(band + [(g, up), (g, down)])
+    beside = [(lax.rem(g + k, n), other) for k in range(n)]
+    corners = [(lax.rem(g + k, n), sibling) for k in (0, 1, n - 1)]
+    everyone = greet(band + beside + corners)
     exchange = Exchange(n, ng, g, y, row_out, row_in, col_out, col_in, row_s, row_r, col_s, col_r)
     lane = iota((8, 128), 1)
     row = iota((1, 128), 1)
@@ -229,14 +297,22 @@
         value = (owner * 32 + by * KX + lax.rem(bx, KX)) * 32 + rank
         code = jnp.where(row == s, jnp.where(owner >= 0, value, -1), code)
     loads[0].wait()
-    pa[0:ROWS, :] = depth_ref[:, 0:128]
-    pb[0:ROWS, 0:EAST] = depth_ref[:, 128:COLS]
-    rims = [jnp.zeros((8, 128), I32) for _ in range(KX)]
+    for half in range(2):
+        dpl[half, 0:16, :] = jnp.zeros((16, 128), F32)
+        dpl[half, 312:UROWS, :] = jnp.zeros((UROWS - 312, 128), F32)
+    wide[...] = jnp.zeros(wide.shape, F32)
+    wide[0:COLS, 0:ROWS] = depth_ref[...].astype(F32)
+    for half in range(2):
+        for third in range(3):
+            turned = wide[128 * half : 128 * half + 128, 128 * third : 128 * third + 128].T
+            rows = min(128, ROWS - 128 * third)
+            dpl[half, TOP + 128 * third : TOP + 128 * third + rows, :] = turned[0:rows]
+    rims = [jnp.zeros((8, 128), F32) for _ in range(KX)]
     ns = []
     for i in range(SPAN_N):
         off = SPAN_E * i % 128
-        a = pa[pl.ds(i, 8, stride=SPAN_N), :]
-        b = pb[pl.ds(i, 8, stride=SPAN_N), :]
+        a = dpl[0, pl.ds(TOP + i, 8, stride=SPAN_N), :]
+        b = dpl[1, pl.ds(TOP + i, 8, stride=SPAN_N), :]
         cells = [a, a, jnp.where(lane < 64, b, a)]
         push = 0 if i < 32 else 1
         first, last = (off + push) % 128, (off + SPAN_E - 1 - push) % 128
@@ -251,39 +327,40 @@
                 jnp.where(lane < SPAN_E, ns[bx], lroll(cells[bx], SPAN_E - SPAN_E * bx))
                 for bx in range(KX)
             ]
+    ns = [v.astype(I32) for v in ns]
     for bx in range(KX):
-        for part, value in enumerate((rims[bx], ns[bx])):
+        for part, value in enumerate((rims[bx].astype(I32), ns[bx])):
             msg[pl.ds(bx * 2 + part, 8, stride=6), :] = value
-    msg[36:37, :] = code
+    msg[IDS : IDS + 1, :] = code
     edge[...] = jnp.zeros((8, 128), I32)
     for bx in range(KX):
+        msg[MIRROR + bx : MIRROR + bx + 1, :] = lroll(lreverse(ns[bx]), -8)[KY - 1 : KY]
         edge[bx : bx + 1, :] = ns[bx][0:1]
         edge[3 + bx : 4 + bx, :] = ns[bx][KY - 1 : KY]
-    zero8 = jnp.zeros((8, 128), F32)
-    for half in range(2):
-        dpl[half, 0:16, :] = jnp.zeros((16, 128), F32)
-        dpl[half, 312:PLANE, :] = jnp.zeros((PLANE - 312, 128), F32)
-    dpl[0, TOP : TOP + ROWS, :] = depth_ref[:, 0:128].astype(F32)
-    dpl[1, TOP : TOP + ROWS, :] = jnp.zeros((ROWS, 128), F32)
-    dpl[1, TOP : TOP + ROWS, 0:EAST] = depth_ref[:, 128:COLS].astype(F32)
+    exchange.pack(0, dpl)
 
     everyone()
-    copies = []
-    for slot, target in ((0, up), (1, down)):
+    near = pltpu.make_async_remote_copy(
+        edge, got, s1.at[0], r1.at[0], device_id=(g, sibling), device_id_type=MESH
+    )
+    near.start()
+    sends = []
+    for k, peer in enumerate(beside):
         copy = pltpu.make_async_remote_copy(
-            edge, got.at[slot], s1.at[slot], r1.at[slot], device_id=(g, target), device_id_type=MESH
-        )
-        copy.start()
-        copies.append(copy)
-    rows = exchange.halo_rows(0, dpl)
-    sends = []
-    for k, peer in enumerate(band):
-        copy = pltpu.make_async_remote_copy(
-            msg.at[pl.ds(0, NEAR)], all_ref.at[g, pl.ds(0, NEAR)], s2.at[k], r2.at[k],
-            device_id=peer, device_id_type=MESH,
+            edge, all_ref.at[g, pl.ds(OTHER, 8)], s3.at[k], r3.at[k], device_id=peer, device_id_type=MESH
         )
         copy.start()
         sends.append(copy)
+    near.wait()
+    msg[SIBLING : SIBLING + 8, :] = got[...]
+    for k, peer in enumerate(band):
+        copy = pltpu.make_async_remote_copy(
+            msg, all_ref.at[g, pl.ds(0, OTHER)], s2.at[k], r2.at[k], device_id=peer, device_id_type=MESH
+        )
+        copy.start()
+        sends.append(copy)
+    halo = exchange.start(0)
+    all_ref[pl.ds(g, 1), 0:OTHER] = msg[...][None]
     gain = jnp.zeros((1, 128), F32)
     for k in range(LEVELS):
         above = dfac_ref[k - 1] if k > 0 else jnp.float32(0)
@@ -295,22 +372,6 @@
         coef[1, k : k + 1, :] = 1.0 / base
         coef[2, k : k + 1, :] = jnp.broadcast_to(above, (1, 128))
         coef[3, k : k + 1, :] = gain
-    for copy in copies:
-        copy.wait()
-    near = edge
-    for bx in range(KX):
-        mirrored = lroll(lreverse(ns[bx]), -8)[KY - 1 : KY]
-        near[bx : bx + 1, :] = jnp.where(y == ng - 1, mirrored, got[1, bx : bx + 1, :])
-        near[3 + bx : 4 + bx, :] = got[0, 3 + bx : 4 + bx, :]
-    for k, peer in enumerate(band):
-        copy = pltpu.make_async_remote_copy(
-            near, all_ref.at[g, pl.ds(NEAR, 8)], s3.at[k], r3.at[k], device_id=peer, device_id_type=MESH
-        )
-        copy.start()
-        sends.append(copy)
-    cols = exchange.halo_cols(0, dpl, rows)
-    all_ref[pl.ds(g, 1), 0:NEAR] = msg[0:NEAR, :][None]
-    all_ref[pl.ds(g, 1), NEAR:STRIP_ROWS] = near[...][None]
     loads[1].wait()
     loads[2].wait()
     for t in range(TILES):
@@ -324,10 +385,11 @@
                 if width < 128:
                     value = jnp.concatenate([value, jnp.zeros((number, 128 - width), kind)], axis=1)
                 dst[place, :] = value
-    exchange.halo_end(0, dpl, cols)
+    exchange.wait(0, halo)
+    exchange.unpack(0, dpl)
     for copy in sends:
         copy.wait()
-    codes = all_ref[:, 36, :]
+    codes = all_ref[:, IDS, :]
     key = codes >> 5
     rank = codes & 31
     source = iota((n, 128), 0)
@@ -464,14 +526,15 @@
     mirrored = lax.rem(mirror, KX)
     folded = by == KY * ng - 1
     inner = byl < KY - 1
+    even = lax.rem(lax.div(by, KY), 2) == 0
     north_dev = jnp.where(folded, lax.div(mirror, KX), dev)
     north_row = jnp.where(
         inner,
         ((byl + 1) * KX + bxl) * 2 + 1,
-        jnp.where(folded, NEAR + mirrored, NEAR + bxl),
+        jnp.where(folded, MIRROR + mirrored, jnp.where(even, SIBLING, OTHER) + bxl),
     )
     north = lroll(strip(north_dev, north_row), -4)
-    south_row = jnp.where(byl > 0, ((byl - 1) * KX + bxl) * 2 + 1, NEAR + 3 + bxl)
+    south_row = jnp.where(byl > 0, ((byl - 1) * KX + bxl) * 2 + 1, jnp.where(even, OTHER, SIBLING) + 3 + bxl)
     south = jnp.where(by > 0, lroll(strip(dev, south_row), -SPAN_E), 0)
     j = jcol[...]
     inside = cell < CELLS
@@ -525,7 +588,8 @@
     y = lax.axis_index("gy")
     band = [(lax.rem(g + k, n), y) for k in range(1, n)]
     column = [(g, lax.rem(y + k, ng)) for k in range(1, ng)]
-    everyone = greet(band + column)
+    corners = [(lax.rem(g + a, n), lax.rem(y + b, ng)) for a in (1, n - 1) for b in (1, ng - 1)]
+    everyone = greet(band + column + corners)
     exchange = Exchange(n, ng, g, y, row_out, row_in, col_out, col_in, row_s, row_r, col_s, col_r)
     lane = iota((8, 128), 1)
     sub = iota((8, 128), 0)
@@ -622,9 +686,6 @@
         return blk[pl.ds(bx * 8 * BLK + row, 8, stride=BLK), :]
 
     rims = [[rows_of(bx, TILES + part) for part in range(2)] for bx in range(KX)]
-    for part in range(2):
-        col_out[0, 0, 8 * part : 8 * part + 8, :] = rims[KX - 1][part]
-        col_out[0, 1, 8 * part : 8 * part + 8, :] = rims[0][part]
     cap_rows = [rows_of(bx, TILES + 2) for bx in range(KX)]
 
     def lay(v):
@@ -633,8 +694,6 @@
 
     souths = lay([lroll(cap_rows[bx], SPAN_E * bx) for bx in range(KX)])
     norths = lay([lroll(cap_rows[bx], SPAN_E * bx - SPAN_E) for bx in range(KX)])
-    waits = exchange.start_rows(0, norths, [sroll(v, 8 - (KY - 1)) for v in norths], souths)
-    col_copies = exchange.start_cols(0)
     for i in range(SPAN_N):
         t, off = SPAN_E * i // 128, SPAN_E * i % 128
         cells = []
@@ -644,6 +703,11 @@
                 value = jnp.where(lane >= off, value, rows_of(bx, t + 1))
             cells.append(lroll(value, SPAN_E * bx - off))
         first, second = lay(cells)
+        second = jnp.where(
+            lane == 60,
+            lroll(rims[KX - 1][i // 32], 61 - SPAN_E - off),
+            jnp.where(lane == 61, lroll(rims[0][i // 32], 61 - off), second),
+        )
         rim = [rims[bx][i // 32] for bx in range(KX)]
         first = first + jnp.where(
             lane == 59,
@@ -662,34 +726,29 @@
             second = second + jnp.where((sub > 0) & (sub < KY), sroll(norths[1], 1), 0.0)
         upl[0, pl.ds(TOP + i, 8, stride=SPAN_N), :] = first
         upl[1, pl.ds(TOP + i, 8, stride=SPAN_N), :] = second
-    below, above = exchange.wait_rows(0, *waits)
-    for copy in col_copies:
-        copy.wait()
     for half in range(2):
-        upl[half, TOP : TOP + 1, :] = upl[half, TOP : TOP + 1, :] + below[half][KY - 1 : KY]
-        end = TOP + ROWS - 1
-        upl[half, end : end + 1, :] = upl[half, end : end + 1, :] + above[half][0:1]
         upl[half, 8:16, :] = zero8
-    for i in range(SPAN_N):
-        off = SPAN_E * i % 128
-        part = slice(8 * (i // 32), 8 * (i // 32) + 8)
-        rows = pl.ds(TOP + i, 8, stride=SPAN_N)
-        west = lroll(col_in[0, 0, part, :], 1 - SPAN_E - off)
-        east = lroll(col_in[0, 1, part, :], COLS - 1 - off)
-        good = sub < KY
-        upl[0, rows, :] = upl[0, rows, :] + jnp.where((lane == 0) & good, west, 0.0)
-        upl[1, rows, :] = upl[1, rows, :] + jnp.where((lane == EAST - 1) & good, east, 0.0)
+    caps = ([v[KY - 1 : KY] for v in norths], [v[0:1] for v in souths])
+    exchange.pack(0, upl, caps)
+    exchange.wait(0, exchange.start(0))
+    exchange.unpack(0, upl, caps)
 
     def begin(t, carry):
         rows = rows_at(t)
-        for half in range(2):
-            rhs = upl[half, rows, :] * (1.0 / LEVELS)
+        a, b = both(upl, rows)
+        a = a + jnp.where(lane_c == 0, lroll(b, -63), 0.0)
+        b = b + jnp.where(
+            lane_c == EAST - 1,
+            lroll(b, EAST - 1 - 62),
+            jnp.where(lane_c == EAST, lroll(b, EAST - 60), jnp.where(lane_c == 127, lroll(b, 127 - 61), 0.0)),
+        )
+        for half, value in enumerate((a, b)):
+            rhs = value * (1.0 / LEVELS)
             qpl[0, half, rows, :] = rhs
             zpl[half, rows, :] = rhs * wts[5, half, rows, :]
         return carry
 
     lax.fori_loop(0, chunks, begin, 0)
-    exchange.halo(1, zpl)
 
     def image(out, scale_next):
         def body(t, carry):
@@ -714,48 +773,30 @@
 
             lax.fori_loop(0, chunks, scale, 0)
 
-    def everywhere(k, parts):
-        red_out[k, 0] = zero8
-        for place, part in enumerate(parts):
-            red_out[k, 0, place : place + 1, :] = jnp.sum(part, axis=0, keepdims=True)
-        for level, (peers, into, sem_s, sem_r, me) in enumerate(
-            ((band, red_x, rx_s, rx_r, g), (column, red_y, ry_s, ry_r, y))
-        ):
-            copies = []
-            for number, peer in enumerate(peers):
-                copy = pltpu.make_async_remote_copy(
-                    red_out.at[k, level], into.at[k, me], sem_s.at[k, number], sem_r.at[k, number],
-                    device_id=peer, device_id_type=MESH,
-                )
-                copy.start()
-                copies.append(copy)
-            into[k, pl.ds(me, 1)] = red_out[k, level][None]
-            for copy in copies:
-                copy.wait()
-            total = jnp.sum(into[k], axis=0)
-            if level == 0:
-                red_out[k, 1] = total
-        total = jnp.sum(total, axis=1, keepdims=True)
-        return [jnp.broadcast_to(total[place : place + 1], (8, 128)) for place in range(len(parts))]
-
     image(1, True)
+    image(2, True)
+    image(3, False)
+
+    def fold3(v):
+        return v[0:8] + v[8:16] + v[16:24]
 
     def first_dots(t, carry):
         rows = rows_at(t)
         a, b = carry
         for half in range(2):
             z = qpl[0, half, rows, :] * wts[6, half, rows, :]
-            a = a + qpl[0, half, rows, :] * z
-            b = b + qpl[1, half, rows, :] * z
+            a = a + fold3(qpl[0, half, rows, :] * z)
+            b = b + fold3(qpl[1, half, rows, :] * z)
         return a, b
 
-    zero_c = jnp.zeros((span, 128), F32)
-    mu = everywhere(0, lax.fori_loop(0, chunks, first_dots, (zero_c, zero_c)))
-    image(2, True)
-    image(3, False)
-    norm = mu[0]
-    ray = mu[1] / norm
-    ray_c = jnp.broadcast_to(ray[0:1], (span, 128))
+    def splat(v):
+        v = jnp.sum(jnp.sum(v, axis=0, keepdims=True), axis=1, keepdims=True)
+        return jnp.broadcast_to(v, (8, 128))
+
+    mass, curve = [splat(v) for v in lax.fori_loop(0, chunks, first_dots, (zero8, zero8))]
+    own_ray = jnp.where(mass > 0, jnp.clip(curve / jnp.where(mass > 0, mass, 1.0), 0.0, 2.0), 0.0)
+    ray_c = jnp.broadcast_to(own_ray[0:1], (span, 128))
+    pairs = ((0, 0), (1, 0), (2, 0), (3, 0), (1, 1), (2, 1), (3, 1), (2, 2), (3, 2))
 
     def shift(t, carry):
         rows = rows_at(t)
@@ -770,17 +811,76 @@
             qpl[1, half, rows, :] = q1
             qpl[2, half, rows, :] = q2
             qpl[3, half, rows, :] = q3
+            q = (w0, q1, q2, q3)
             inverse = wts[6, half, rows, :]
-            z1 = q1 * inverse
-            z2 = q2 * inverse
-            c[0] = c[0] + w0 * z1
-            c[1] = c[1] + q1 * z1
-            c[2] = c[2] + q2 * z1
-            c[3] = c[3] + q2 * z2
-            c[4] = c[4] + q3 * z2
+            z = [v * inverse for v in q[0:3]]
+            for place, (i, j) in enumerate(pairs):
+                c[place] = c[place] + fold3(q[i] * z[j])
         return tuple(c)
 
-    moment = everywhere(1, lax.fori_loop(0, chunks, shift, (zero_c,) * 5))
+    sums = lax.fori_loop(0, chunks, shift, (zero8,) * len(pairs))
+    red_out[0, 0:1, :] = own_ray[0:1]
+    red_out[0, 1:2, :] = mass[0:1]
+    for place, part in enumerate(sums):
+        red_out[0, 2 + place : 3 + place, :] = jnp.sum(part, axis=0, keepdims=True)
+    red_out[0, 11:16, :] = jnp.zeros((5, 128), F32)
+    for level, (peers, into, sem_s, sem_r, me) in enumerate(
+        ((band, red_x, rx_s, rx_r, g), (column, red_y, ry_s, ry_r, y))
+    ):
+        place = pl.ds(pl.multiple_of(me * 16, 8), 16)
+        copies = []
+        for number, peer in enumerate(peers):
+            copy = pltpu.make_async_remote_copy(
+                red_out.at[level], into.at[place], sem_s.at[number], sem_r.at[number],
+                device_id=peer, device_id_type=MESH,
+            )
+            copy.start()
+            copies.append(copy)
+        into[place, :] = red_out[level]
+        for copy in copies:
+            copy.wait()
+        count = len(peers) + 1
+        ray, mass, *old = [into[pl.ds(m, count, stride=16), :] for m in range(2 + len(pairs))]
+        total = jnp.sum(mass, axis=0, keepdims=True)
+        common = jnp.sum(ray * mass, axis=0, keepdims=True) / total
+        common = jnp.where(total > 0, common, 0.0)
+        d = ray - common
+        terms = [[None] * 4 for _ in range(4)]
+        for i, c in enumerate(((1,), (1, 1), (1, 2, 1), (1, 3, 3, 1))):
+            for j in range(i + 1):
+                power = jnp.full(d.shape, float(c[j]), F32)
+                for _ in range(i - j):
+                    power = power * d
+                terms[i][j] = power
+        gram = dict(zip(pairs, old))
+
+        def entry(i, j):
+            return gram[(i, j)] if i >= j else gram[(j, i)]
+
+        new = []
+        for i, j in pairs:
+            value = None
+            for a in range(i + 1):
+                for b in range(j + 1):
+                    term = entry(a, b)
+                    if a < i:
+                        term = term * terms[i][a]
+                    if b < j:
+                        term = term * terms[j][b]
+                    value = term if value is None else value + term
+            new.append(jnp.sum(value, axis=0, keepdims=True))
+        if level == 0:
+            red_out[1, 0:1, :] = common
+            red_out[1, 1:2, :] = total
+            for number, part in enumerate(new):
+                red_out[1, 2 + number : 3 + number, :] = part
+            red_out[1, 11:16, :] = jnp.zeros((5, 128), F32)
+    ray = jnp.broadcast_to(common, (8, 128))
+    moment = {
+        pair: jnp.broadcast_to(jnp.sum(part, axis=1, keepdims=True), (8, 128)) for pair, part in zip(pairs, new)
+    }
+    norm = moment[(0, 0)]
+    moment = [moment[pair] for pair in ((1, 0), (1, 1), (2, 1), (2, 2), (3, 2))]
     one = jnp.ones((8, 128), F32)
     scale = one / norm
     c = [one] + [m * scale for m in moment]
@@ -811,6 +911,16 @@
         pi = [rho[i] + beta * pi[i] for i in range(3)]
         gamma = gamma_new
 
+    d = own_ray - ray
+    d2 = d * d
+    rho = [
+        rho[0] + d * rho[1] + d2 * rho[2] + d2 * d * rho[3],
+        rho[1] + 2.0 * d * rho[2] + 3.0 * d2 * rho[3],
+        rho[2] + 3.0 * d * rho[3],
+        rho[3],
+    ]
+    xs = [xs[0] + d * xs[1] + d2 * xs[2], xs[1] + 2.0 * d * xs[2], xs[2]]
+
     def finish(first, size):
         rows = pl.ds(TOP + first, size)
         out = pl.ds(first, size)
@@ -845,23 +955,22 @@
         functools.partial(strips_kernel, n, ng, (SLOTS + n - 1) // n),
         out_shape=(
             jax.ShapeDtypeStruct((n, STRIP_ROWS, 128), I32), jax.ShapeDtypeStruct((24, 128), I32),
-            jax.ShapeDtypeStruct((2, PLANE, 128), F32), jax.ShapeDtypeStruct((4, 32, 128), F32),
+            jax.ShapeDtypeStruct((2, UROWS, 128), F32), jax.ShapeDtypeStruct((4, 32, 128), F32),
             jax.ShapeDtypeStruct(flat, I32), jax.ShapeDtypeStruct(flat, F32),
         ),
         in_specs=[smem, smem, hbm, hbm, hbm],
         out_specs=(vmem,) * 6,
         scratch_shapes=[
-            VMEM((ROWS, COLS), I32), VMEM((SLOTS, CELLS), I32), VMEM((SLOTS, CELLS), F32),
-            VMEM((400, 128), I32), VMEM((400, 128), I32), VMEM((48, 128), I32), VMEM((8, 128), I32),
-            VMEM((2, 8, 128), I32),
-            VMEM((1, 2, 2, 8, 128), F32), VMEM((1, 2, 2, 8, 128), F32),
+            VMEM((COLS, ROWS), I32), VMEM((SLOTS, CELLS), I32), VMEM((SLOTS, CELLS), F32),
+            VMEM((256, 384), F32), VMEM((48, 128), I32), VMEM((8, 128), I32), VMEM((8, 128), I32),
+            VMEM((1, 2, 2, 8, 128), F32), VMEM((1, 2, 3, 2, 8, 128), F32),
             VMEM((1, 2, 16, 128), F32), VMEM((1, 2, 16, 128), F32),
-            dma((3,)), dma((2,)), dma((2,)), dma((n,)), dma((n,)), dma((n,)), dma((n,)),
-            dma((1, 2)), dma((1, 2)), dma((1, 2)), dma((1, 2)),
+            dma((3,)), dma((1,)), dma((1,)), dma((n,)), dma((n,)), dma((n,)), dma((n,)),
+            dma((1, 2, 3)), dma((1, 2, 3)), dma((1, 2)), dma((1, 2)),
         ],
         compiler_params=pltpu.CompilerParams(collective_id=0, has_side_effects=True, vmem_limit_bytes=BIG),
         name="strips",
-    )(ids, dfac, grid_depth, slot_depth, flux)
+    )(ids, dfac, grid_depth.T, slot_depth, flux)
 
 
 def columns_call(n, ng, heat, salt, ids, coef, fflat, nflat, strips):
@@ -913,11 +1022,11 @@
             VMEM((n, message_rows(cap), 128), F32), VMEM((KX * 8 * BLK, 128), F32),
             VMEM((2, UROWS, 128), F32), VMEM(plane, F32),
             VMEM((7,) + plane, F32), VMEM((4,) + plane, F32),
-            VMEM((2, 2, 2, 8, 128), F32), VMEM((2, 2, 2, 8, 128), F32),
-            VMEM((2, 2, 16, 128), F32), VMEM((2, 2, 16, 128), F32),
-            VMEM((2, 2, 8, 128), F32), VMEM((2, n, 8, 128), F32), VMEM((2, ng, 8, 128), F32),
-            dma, dma((n,)), dma((n,)), dma((2, 2)), dma((2, 2)), dma((2, 2)), dma((2, 2)),
-            dma((2, n)), dma((2, n)), dma((2, ng)), dma((2, ng)),
+            VMEM((1, 2, 2, 8, 128), F32), VMEM((1, 2, 3, 2, 8, 128), F32),
+            VMEM((1, 2, 16, 128), F32), VMEM((1, 2, 16, 128), F32),
+            VMEM((2, 16, 128), F32), VMEM((n * 16, 128), F32), VMEM((ng * 16, 128), F32),
+            dma, dma((n,)), dma((n,)), dma((1, 2, 3)), dma((1, 2, 3)), dma((1, 2)), dma((1, 2)),
+            dma((n,)), dma((n,)), dma((ng,)), dma((ng,)),
         ],
         compiler_params=pltpu.CompilerParams(collective_id=1, has_side_effects=True, vmem_limit_bytes=BIG),
         name="barotropic",

time: 88.9 us -> 77.1 us (0.87)
  Pallas kernels: 82.4 us -> 72.5 us
  local copies, waits for them, and re-layouts: 5.47 us -> 3.65 us
    pallas_call x1, Pallas kernels: 49.1 us -> 35.7 us  [barotropic_call(): pl.pallas_call(functools.partial(barotropic_kernel, n, ng, cap), out_shap...]
    pallas_call x1, Pallas kernels: 16.9 us -> 20.3 us  [strips_call(): pl.pallas_call(functools.partial(strips_kernel, n, ng, (SLOTS + n - 1) //...]
    unnamed x3 -> x2, local copies, waits for them, and re-layouts: 5.47 us -> 3.65 us
where the time goes in v3:
time: 77.1 us; the launch traced here: 76.8 us
  Pallas kernels  72.5 us (94%)
  local copies, waits for them, and re-layouts  3.65 us (5%)
    pallas_call x1, Pallas kernels, barotropic_call(): pl.pallas_call(functools.partial(barotropic_kernel, n, ng, cap), out_shap...  35.7 us
    pallas_call x1, Pallas kernels, strips_call(): pl.pallas_call(functools.partial(strips_kernel, n, ng, (SLOTS + n - 1) //...  20.3 us
    pallas_call x1, Pallas kernels, columns_call(): pl.pallas_call(functools.partial(columns_kernel, n, ng, cap), grid=(SLOTS...  16.5 us
    unnamed x2, local copies, waits for them, and re-layouts  3.65 us

profile of v3, /device:TPU:1, one launch (start us, length us, event | category | flops | bytes accessed | tf_op | source)
XLA Modules:
  0.0 76.8 jit_solution(4740972599011245620)
XLA Ops:
  0.6 20.3 %strips.1 = (s32[16,56,128]{2,1,0:T(8,128)}, s32[24,128]{1,0:T(8,128)}, f32[2,416,128]{2,1,0:T(8,128)}, f32[4,32,128]{2,1,0:T(8,128)}, s32[432,128]{1,0:T(8,128)}, /*index=5*/f32[432,128]{1,0:T(8,128)}) custom-call(s32[18]{0:T(128)} %ids_ref.3, f32[29]{0:T(128)} %dfac_ref.1, s32[180,300]{1,0:T(8,128)} %bitcast.1, s32[18,3000]{1,0:T(8,128)} %slot_hbm.1, ...), custom_call_target="tpu_custom_call" | custom-call | tf_op jit(solution)/shard_map/strips/pallas_call | solution.py:954
  21.0 16.5 %columns.1 = (f32[18,30,3000]{2,1,0:T(8,128)}, f32[18,30,3000]{2,1,0:T(8,128)}, f32[16,56,128]{2,1,0:T(8,128)}) custom-call(s32[18]{0:T(128)} %ids_ref.3, f32[4,32,128]{2,1,0:T(8,128)} %get-tuple-element.15.coef, f32[432,128]{1,0:T(8,128)} %get-tuple-element.16.fflat, s32[432,128]{1,0:T(8,128)} %get-tuple-element.17.nflat, ...), custom_call_target="tpu_custom_call" | custom-call | tf_op jit(solution)/shard_map/columns/pallas_call | solution.py:985
  37.5 35.7 %barotropic.1 = (f32[300,180]{1,0:T(8,128)}, f32[300,180]{1,0:T(8,128)}) custom-call(s32[24,128]{1,0:T(8,128)} %get-tuple-element.21.tab_ref, f32[2,416,128]{2,1,0:T(8,128)} %get-tuple-element.22.dpl, f32[16,56,128]{2,1,0:T(8,128)} %get-tuple-element.23.msg_ref), custom_call_target="tpu_custom_call" | custom-call | tf_op jit(solution)/shard_map/barotropic/pallas_call | solution.py:1016
  73.1 1.8 %copy.11 = f32[300,180]{0,1:T(8,128)} copy(f32[300,180]{1,0:T(8,128)} %get-tuple-element.28) | data formatting | bytes 432000
  74.9 1.8 %copy.12 = f32[300,180]{0,1:T(8,128)} copy(f32[300,180]{1,0:T(8,128)} %get-tuple-element.29) | data formatting | bytes 432000

commit v4 on v3

--- a/solution.py
+++ b/solution.py
@@ -581,7 +581,7 @@
 
 
 def barotropic_kernel(n, ng, cap, tab_ref, dpl, msg_ref, height_ref, misfit_ref,
-                      recv, blk, upl, zpl, wts, qpl, row_out, row_in, col_out, col_in,
+                      recv, blk, upl, zs, spare, wts, qpl, row_out, row_in, col_out, col_in,
                       red_out, red_x, red_y, own_sem, a2a_s, a2a_r, row_s, row_r, col_s, col_r,
                       rx_s, rx_r, ry_s, ry_r):
     g = lax.axis_index("gx")
@@ -595,7 +595,7 @@
     sub = iota((8, 128), 0)
     zero8 = jnp.zeros((8, 128), F32)
     for half in range(2):
-        for ref in (zpl, qpl.at[0], qpl.at[1], qpl.at[2], qpl.at[3]):
+        for ref in (zs.at[0], zs.at[1], zs.at[2]):
             ref[half, 0:8, :] = zero8
             ref[half, 320:PLANE, :] = zero8
 
@@ -638,7 +638,7 @@
             wts[6, half, rows, :] = jnp.where(inside, inverse, 0.0)
         return carry
 
-    lax.fori_loop(0, chunks, weigh, 0)
+    lax.fori_loop(0, chunks, weigh, 0, unroll=True)
 
     everyone()
     own = pltpu.make_async_copy(msg_ref.at[g], recv.at[g], own_sem)
@@ -745,37 +745,32 @@
         for half, value in enumerate((a, b)):
             rhs = value * (1.0 / LEVELS)
             qpl[0, half, rows, :] = rhs
-            zpl[half, rows, :] = rhs * wts[5, half, rows, :]
+            zs[0, half, rows, :] = rhs * wts[5, half, rows, :]
         return carry
 
-    lax.fori_loop(0, chunks, begin, 0)
-
-    def image(out, scale_next):
+    lax.fori_loop(0, chunks, begin, 0, unroll=True)
+
+    def image(out):
+        z = zs.at[out - 1]
+
         def body(t, carry):
             rows = rows_at(t)
-            v = both(zpl, rows)
-            beside = (from_east(v), from_west(v), both(zpl, rows_at(t, 1)), both(zpl, rows_at(t, -1)))
+            v = both(z, rows)
+            beside = (from_east(v), from_west(v), both(z, rows_at(t, 1)), both(z, rows_at(t, -1)))
             for half in range(2):
                 result = wts[4, half, rows, :] * v[half]
                 for side in range(4):
                     result = result + wts[side, half, rows, :] * (v[half] - beside[side][half])
                 qpl[out, half, rows, :] = result
+                if out < 3:
+                    zs[out, half, rows, :] = result * wts[5, half, rows, :]
             return carry
 
-        lax.fori_loop(0, chunks, body, 0)
-        if scale_next:
-
-            def scale(t, carry):
-                rows = rows_at(t)
-                for half in range(2):
-                    zpl[half, rows, :] = qpl[out, half, rows, :] * wts[5, half, rows, :]
-                return carry
-
-            lax.fori_loop(0, chunks, scale, 0)
-
-    image(1, True)
-    image(2, True)
-    image(3, False)
+        lax.fori_loop(0, chunks, body, 0, unroll=True)
+
+    image(1)
+    image(2)
+    image(3)
 
     def fold3(v):
         return v[0:8] + v[8:16] + v[16:24]
@@ -793,7 +788,7 @@
         v = jnp.sum(jnp.sum(v, axis=0, keepdims=True), axis=1, keepdims=True)
         return jnp.broadcast_to(v, (8, 128))
 
-    mass, curve = [splat(v) for v in lax.fori_loop(0, chunks, first_dots, (zero8, zero8))]
+    mass, curve = [splat(v) for v in lax.fori_loop(0, chunks, first_dots, (zero8, zero8), unroll=True)]
     own_ray = jnp.where(mass > 0, jnp.clip(curve / jnp.where(mass > 0, mass, 1.0), 0.0, 2.0), 0.0)
     ray_c = jnp.broadcast_to(own_ray[0:1], (span, 128))
     pairs = ((0, 0), (1, 0), (2, 0), (3, 0), (1, 1), (2, 1), (3, 1), (2, 2), (3, 2))
@@ -818,7 +813,7 @@
                 c[place] = c[place] + fold3(q[i] * z[j])
         return tuple(c)
 
-    sums = lax.fori_loop(0, chunks, shift, (zero8,) * len(pairs))
+    sums = lax.fori_loop(0, chunks, shift, (zero8,) * len(pairs), unroll=True)
     red_out[0, 0:1, :] = own_ray[0:1]
     red_out[0, 1:2, :] = mass[0:1]
     for place, part in enumerate(sums):
@@ -923,26 +918,32 @@
 
     def finish(first, size):
         rows = pl.ds(TOP + first, size)
-        out = pl.ds(first, size)
         x = [jnp.broadcast_to(v[0:1], (size, 128)) for v in xs]
         r = [jnp.broadcast_to(v[0:1], (size, 128)) for v in rho]
         for half in range(2):
             q = [qpl[j, half, rows, :] for j in range(4)]
             high = (x[0] * q[0] + x[1] * q[1] + x[2] * q[2]) * wts[5, half, rows, :]
             rest = r[0] * q[0] + r[1] * q[1] + r[2] * q[2] + r[3] * q[3]
-            if half == 0:
-                height_ref[out, 0:128] = high
-                misfit_ref[out, 0:128] = rest
-            else:
-                height_ref[out, 128:COLS] = high[:, 0:EAST]
-                misfit_ref[out, 128:COLS] = rest[:, 0:EAST]
+            spare[half, rows, :] = high
+            upl[half, rows, :] = rest
 
     def finish_chunk(t, carry):
         finish(pl.multiple_of(t * span, 8), span)
         return carry
 
-    lax.fori_loop(0, ROWS // span, finish_chunk, 0)
+    lax.fori_loop(0, ROWS // span, finish_chunk, 0, unroll=True)
     finish(ROWS // span * span, ROWS % span)
+    for source, out_ref in ((spare, height_ref), (upl, misfit_ref)):
+        for half in range(2):
+            for third in range(3):
+                turned = source[half, TOP + 128 * third : TOP + 128 * third + 128, :].T
+                tall, wide = min(128, COLS - 128 * half), min(128, ROWS - 128 * third)
+                out_ref[128 * half : 128 * half + tall, 128 * third : 128 * third + wide] = turned[0:tall, 0:wide]
+
+
+def place_kernel(a_ref, b_ref, a_out, b_out):
+    a_out[...] = a_ref[...]
+    b_out[...] = b_ref[...]
 
 
 def strips_call(n, ng, flux, dfac, ids, slot_depth, grid_depth):
@@ -1011,7 +1012,7 @@
     cap = (SLOTS + n - 1) // n
     vmem = pl.BlockSpec(memory_space=VMEM)
     dma = pltpu.SemaphoreType.DMA
-    field = jax.ShapeDtypeStruct((ROWS, COLS), F32)
+    field = jax.ShapeDtypeStruct((COLS, ROWS), F32)
     plane = (2, PLANE, 128)
     return pl.pallas_call(
         functools.partial(barotropic_kernel, n, ng, cap),
@@ -1020,7 +1021,7 @@
         out_specs=(vmem, vmem),
         scratch_shapes=[
             VMEM((n, message_rows(cap), 128), F32), VMEM((KX * 8 * BLK, 128), F32),
-            VMEM((2, UROWS, 128), F32), VMEM(plane, F32),
+            VMEM((2, UROWS, 128), F32), VMEM((3,) + plane, F32), VMEM((2, UROWS, 128), F32),
             VMEM((7,) + plane, F32), VMEM((4,) + plane, F32),
             VMEM((1, 2, 2, 8, 128), F32), VMEM((1, 2, 3, 2, 8, 128), F32),
             VMEM((1, 2, 16, 128), F32), VMEM((1, 2, 16, 128), F32),
@@ -1037,7 +1038,12 @@
     strips, table, depths, coef, nflat, fflat = strips_call(n, ng, flux, dfac, ids, slot_depth, grid_depth)
     heat_new, salt_new, msg = columns_call(n, ng, heat, salt, ids, coef, fflat, nflat, strips)
     height, misfit = barotropic_call(n, ng, table, depths, msg)
-    return heat_new, salt_new, height, misfit
+    vmem = pl.BlockSpec(memory_space=VMEM)
+    field = jax.ShapeDtypeStruct((COLS, ROWS), F32)
+    height, misfit = pl.pallas_call(
+        place_kernel, out_shape=(field, field), in_specs=[vmem, vmem], out_specs=(vmem, vmem), name="place"
+    )(height, misfit)
+    return heat_new, salt_new, height.T, misfit.T
 
 
 def solution(mesh):

time: 77.1 us -> 71.1 us (0.922)
  local copies, waits for them, and re-layouts: 3.65 us -> 0 us
  Pallas kernels: 72.5 us -> 70.2 us
    pallas_call x1, Pallas kernels: 35.7 us -> 31.5 us  [barotropic_call(): pl.pallas_call(functools.partial(barotropic_kernel, n, ng, cap), out_shap...]
    unnamed x2 -> x0, local copies, waits for them, and re-layouts: 3.65 us -> none
    pallas_call x0 -> x1, Pallas kernels: none -> 1.87 us  [on_device(): pl.pallas_call(place_kernel, out_shape=(field, field), in_specs=[vmem, vm...]
where the time goes in v4:
time: 71.1 us; the launch traced here: 70.9 us
  Pallas kernels  70.2 us (99%)
    pallas_call x1, Pallas kernels, barotropic_call(): pl.pallas_call(functools.partial(barotropic_kernel, n, ng, cap), out_shap...  31.5 us
    pallas_call x1, Pallas kernels, strips_call(): pl.pallas_call(functools.partial(strips_kernel, n, ng, (SLOTS + n - 1) //...  20.3 us
    pallas_call x1, Pallas kernels, columns_call(): pl.pallas_call(functools.partial(columns_kernel, n, ng, cap), grid=(SLOTS...  16.5 us
    pallas_call x1, Pallas kernels, on_device(): pl.pallas_call(place_kernel, out_shape=(field, field), in_specs=[vmem, vm...  1.87 us

profile of v4, /device:TPU:1, one launch (start us, length us, event | category | flops | bytes accessed | tf_op | source)
XLA Modules:
  0.0 70.9 jit_solution(17234106607006245827)
XLA Ops:
  0.6 20.3 %strips.1 = (s32[16,56,128]{2,1,0:T(8,128)}, s32[24,128]{1,0:T(8,128)}, f32[2,416,128]{2,1,0:T(8,128)}, f32[4,32,128]{2,1,0:T(8,128)}, s32[432,128]{1,0:T(8,128)}, /*index=5*/f32[432,128]{1,0:T(8,128)}) custom-call(s32[18]{0:T(128)} %ids_ref.3, f32[29]{0:T(128)} %dfac_ref.1, s32[180,300]{1,0:T(8,128)} %bitcast.3, s32[18,3000]{1,0:T(8,128)} %slot_hbm.1, ...), custom_call_target="tpu_custom_call" | custom-call | tf_op jit(solution)/shard_map/strips/pallas_call | solution.py:955
  21.0 16.5 %columns.1 = (f32[18,30,3000]{2,1,0:T(8,128)}, f32[18,30,3000]{2,1,0:T(8,128)}, f32[16,56,128]{2,1,0:T(8,128)}) custom-call(s32[18]{0:T(128)} %ids_ref.3, f32[4,32,128]{2,1,0:T(8,128)} %get-tuple-element.17.coef, f32[432,128]{1,0:T(8,128)} %get-tuple-element.18.fflat, s32[432,128]{1,0:T(8,128)} %get-tuple-element.19.nflat, ...), custom_call_target="tpu_custom_call" | custom-call | tf_op jit(solution)/shard_map/columns/pallas_call | solution.py:986
  37.4 31.5 %barotropic.1 = (f32[180,300]{1,0:T(8,128)}, f32[180,300]{1,0:T(8,128)}) custom-call(s32[24,128]{1,0:T(8,128)} %get-tuple-element.23.tab_ref, f32[2,416,128]{2,1,0:T(8,128)} %get-tuple-element.24.dpl, f32[16,56,128]{2,1,0:T(8,128)} %get-tuple-element.25.msg_ref), custom_call_target="tpu_custom_call" | custom-call | tf_op jit(solution)/shard_map/barotropic/pallas_call | solution.py:1017
  69.0 1.9 %place.1 = (f32[180,300]{1,0:T(8,128)}, f32[180,300]{1,0:T(8,128)}) custom-call(f32[180,300]{1,0:T(8,128)} %get-tuple-element.26.a_ref, f32[180,300]{1,0:T(8,128)} %get-tuple-element.27.b_ref), custom_call_target="tpu_custom_call" | custom-call | tf_op jit(solution)/shard_map/place/pallas_call | solution.py:1043
